TPU v7x, 32 devices: a whole 2x2x4 slice. The times are simulated.
32 devices in a mesh: region: 8 (over y, x, core), row: 4 (over z).
Axes of the slice: x: 2, y: 2, z: 4, core: 2. Of those that a mesh axis runs over, the one named last changes fastest.
Arguments:
- inputs: bfloat16 [12, 16384, 227], P('row', 'region'), may hold values from -6 to 6
- targets: bfloat16 [12, 16384, 227], P('row', 'region'), may hold values from -6 to 6
- valid_steps: int32 [12, 16384], P('row', 'region'), may hold values from 0 to 1, as said below
- var_weights: float32 [227], replicated, may hold values from 0.3 to 3
- grid_to_mesh: int32 [4096, 4], P('region'), may hold values from 0 to 2047
- mesh_edges: int32 [4096, 8], P('region'), may hold values from 0 to 639
- send_rows: int32 [1024], P('region'), may hold values from 0 to 511
- mesh_to_grid: int32 [16384, 3], P('region'), may hold values from 0 to 511
- date_index: int32 [12], P('row'), may hold values from 0 to 7
- matrices: float32 [7, 512, 512], P(None, 'row'), may hold values from -0.25 to 0.25
- matrices_momentum: float32 [7, 512, 512], P(None, 'row'), may hold values from -0.125 to 0.125
- in_proj: float32 [227, 512], P(None, 'row'), may hold values from -0.375 to 0.375
- in_first: float32 [227, 512], P(None, 'row'), may hold values from -0.015625 to 0.015625
- in_second: float32 [227, 512], P(None, 'row'), may hold values from 2.1362305e-06 to 3.4077962e-05
- out_proj: float32 [512, 227], P('row'), may hold values from -0.25 to 0.25
- out_first: float32 [512, 227], P('row'), may hold values from -0.015625 to 0.015625
- out_second: float32 [512, 227], P('row'), may hold values from 2.1362305e-06 to 3.4077962e-05
- norm_gains: float32 [3, 512], P(None, 'row'), may hold values from 0.5 to 1.5
- gains_first: float32 [3, 512], P(None, 'row'), may hold values from -0.046875 to 0.046875
- gains_second: float32 [3, 512], P(None, 'row'), may hold values from 1.93278e-05 to 0.00030517578
- date_table: float32 [8, 512], P(None, 'row'), may hold values from -3 to 3
- date_first: float32 [8, 512], P(None, 'row'), may hold values from -0.046875 to 0.046875
- date_second: float32 [8, 512], P(None, 'row'), may hold values from 1.93278e-05 to 0.00030517578
Outputs:
- new_matrices: float32 [7, 512, 512], P(None, 'row')
- new_momentum: float32 [7, 512, 512], P(None, 'row')
- new_in_proj: float32 [227, 512], P(None, 'row')
- new_in_first: float32 [227, 512], P(None, 'row')
- new_in_second: float32 [227, 512], P(None, 'row')
- new_out_proj: float32 [512, 227], P('row')
- new_out_first: float32 [512, 227], P('row')
- new_out_second: float32 [512, 227], P('row')
- new_gains: float32 [3, 512], P(None, 'row')
- new_gains_first: float32 [3, 512], P(None, 'row')
- new_gains_second: float32 [3, 512], P(None, 'row')
- new_dates: float32 [8, 512], P(None, 'row')
- new_date_first: float32 [8, 512], P(None, 'row')
- new_date_second: float32 [8, 512], P(None, 'row')
- loss_sum: float32 [], replicated
- valid_count: float32 [], replicated
Inputs may be any that keep to these rules, and one draw needn't show every extreme that they name: `valid_steps`: each value is 0 or 1; the share of ones varies over members and grid points. `grid_to_mesh`: indices of grid points within the mesh node's own region. `mesh_edges`: rows below 512 are the region's own mesh nodes; the next 64 rows come from the previous region, the last 64 from the next one, cyclically. `send_rows`: within a region's 2 * 64 slots, the first 64 go to the previous region and the last 64 to the next one; a row may be sent several times. `mesh_to_grid`: indices of mesh nodes within the grid point's own region.
All inputs are finite; a program needn't handle non-finite values.
Results may differ from a plain program's by a relative error of at most 0.0011.
The roundings to bfloat16 on the way count: a program that leaves them out, or rounds other values in their place, can miss the bound.
Values may be sent and summed in bfloat16 or wider, within the bound.
A program may use at most 320 MiB of HBM per device.

v0:
```python
from functools import partial

import jax
import jax.numpy as jnp
from jax import lax
from jax.sharding import PartitionSpec as P

NS_ITERS = 2
STEP = 10


HIGHEST = lax.Precision.HIGHEST
NS_COEFFS = (3.4445, -4.775, 2.0315)
MUON_RATE = 0.8
MUON_MOMENTUM = 0.95
MATRIX_RATE = 0.05
VECTOR_RATE = 0.2
BETA_ONE = 0.9
BETA_TWO = 0.95
WEIGHT_DECAY = 0.01


def with_halo(block, sides, width):
    for axis, dim in sides:
        count = lax.axis_size(axis)
        forward = [(i, i + 1) for i in range(count - 1)]
        forward.append((count - 1, 0))
        backward = [(target, source) for source, target in forward]
        low = lax.ppermute(
            lax.slice_in_dim(block, block.shape[dim] - width, None, axis=dim), axis, forward
        )
        high = lax.ppermute(lax.slice_in_dim(block, 0, width, axis=dim), axis, backward)
        block = jnp.concatenate([low, block, high], axis=dim)
    return block


def round_low(values):
    rounded = values.astype(jnp.bfloat16).astype(jnp.float32)
    return values + lax.stop_gradient(rounded - values)


def product(left_side, right_side):
    return jnp.dot(left_side, right_side, precision=HIGHEST)


def norm_rows(values, gain_row):
    centred = values - jnp.mean(values, axis=-1, keepdims=True)
    spread = jnp.mean(centred * centred, axis=-1, keepdims=True)
    return centred * lax.rsqrt(spread + 1e-05) * gain_row


def branch_mlp(values, first_matrix, second_matrix, gain_row):
    hidden = round_low(jax.nn.silu(product(round_low(values), first_matrix)))
    return norm_rows(product(hidden, second_matrix), gain_row)


def encode(params, inputs, date_row, grid_to_mesh):
    matrices, in_proj, out_proj, norm_gains, date_table = params
    grid_start = product(inputs, in_proj) + date_table[date_row]
    agg_start = jnp.mean(grid_start[grid_to_mesh], axis=1)
    mesh_one = agg_start + branch_mlp(agg_start, matrices[0], matrices[1], norm_gains[0])
    return (mesh_one, grid_start)


def decode(
    params,
    mesh_one,
    left_rows,
    right_rows,
    grid_start,
    inputs,
    targets,
    valid_row,
    var_weights,
    mesh_edges,
    mesh_to_grid,
):
    matrices, in_proj, out_proj, norm_gains, date_table = params
    sent = round_low(mesh_one)
    extended = jnp.concatenate([sent, left_rows, right_rows], axis=0)
    senders = product(extended, matrices[2])
    receivers = product(sent, matrices[3])
    pre_act = senders[mesh_edges] + receivers[:, None, :]
    hidden = round_low(jax.nn.silu(pre_act))
    agg_mesh = product(jnp.mean(hidden, axis=1), matrices[4])
    mesh_two = mesh_one + norm_rows(agg_mesh, norm_gains[1])
    decoded = jnp.mean(mesh_two[mesh_to_grid], axis=1)
    grid_one = grid_start + branch_mlp(decoded, matrices[5], matrices[6], norm_gains[2])
    predicted = inputs + product(round_low(grid_one), out_proj)
    misfit = predicted - targets
    return jnp.sum(valid_row[:, None] * var_weights[None, :] * misfit * misfit)


def collect(matrices, in_proj, out_proj, norm_gains, date_table):
    pieces = (
        lax.all_gather(matrices.astype(jnp.bfloat16), "row", axis=1, tiled=True),
        lax.all_gather(in_proj.astype(jnp.bfloat16), "row", axis=1, tiled=True),
        lax.all_gather(out_proj.astype(jnp.bfloat16), "row", axis=0, tiled=True),
        lax.all_gather(norm_gains.astype(jnp.bfloat16), "row", axis=1, tiled=True),
        lax.all_gather(date_table.astype(jnp.bfloat16), "row", axis=1, tiled=True),
    )
    return tuple((piece.astype(jnp.float32) for piece in pieces))


def gram_sum(block):
    return lax.psum(
        jnp.einsum("mrk,mrl->mkl", block, block, precision=HIGHEST).astype(jnp.bfloat16), "row"
    ).astype(jnp.float32)


def sweep_step(current, gram_matrix):
    square = jnp.einsum("mkj,mjl->mkl", gram_matrix, gram_matrix, precision=HIGHEST)
    mixing = NS_COEFFS[1] * gram_matrix + NS_COEFFS[2] * square
    return NS_COEFFS[0] * current + jnp.einsum("mrk,mkl->mrl", current, mixing, precision=HIGHEST)


def adam_update(weight, gradient, first_moment, second_moment, step_rate, decay_rate):
    first_new = BETA_ONE * first_moment + (1.0 - BETA_ONE) * gradient
    second_new = BETA_TWO * second_moment + (1.0 - BETA_TWO) * gradient * gradient
    unbiased_one = first_new / (1.0 - BETA_ONE**STEP)
    unbiased_two = second_new / (1.0 - BETA_TWO**STEP)
    weight_new = weight * (1.0 - step_rate * decay_rate) - step_rate * unbiased_one / (
        jnp.sqrt(unbiased_two) + 1e-08
    )
    return (weight_new, first_new, second_new)


def body(
    inputs,
    targets,
    valid_steps,
    var_weights,
    grid_to_mesh,
    mesh_edges,
    send_rows,
    mesh_to_grid,
    date_index,
    matrices,
    matrices_momentum,
    in_proj,
    in_first,
    in_second,
    out_proj,
    out_first,
    out_second,
    norm_gains,
    gains_first,
    gains_second,
    date_table,
    date_first,
    date_second,
):
    halo_rows = send_rows.shape[0] // 2
    masks = valid_steps.astype(jnp.float32)
    valid_count = lax.psum(jnp.sum(masks), ("region", "row"))
    cotangent = 1.0 / valid_count
    owned = (matrices, in_proj, out_proj, norm_gains, date_table)
    totals = None
    loss_local = jnp.zeros((), jnp.float32)
    for member in range(inputs.shape[0]):
        params = collect(*owned)
        data_in = inputs[member].astype(jnp.float32)
        data_out = targets[member].astype(jnp.float32)
        encoder = partial(
            encode, inputs=data_in, date_row=date_index[member], grid_to_mesh=grid_to_mesh
        )
        (mesh_one, grid_start), encode_back = jax.vjp(encoder, params)
        buffer = mesh_one[send_rows].astype(jnp.bfloat16)
        padded = with_halo(buffer, (("region", 0),), halo_rows)
        left_rows = padded[:halo_rows].astype(jnp.float32)
        right_rows = padded[-halo_rows:].astype(jnp.float32)
        decoder = partial(
            decode,
            inputs=data_in,
            targets=data_out,
            valid_row=masks[member],
            var_weights=var_weights,
            mesh_edges=mesh_edges,
            mesh_to_grid=mesh_to_grid,
        )
        loss_part, decode_back = jax.vjp(
            decoder, params, mesh_one, left_rows, right_rows, grid_start
        )
        g_params, g_mesh, g_left, g_right, g_grid = decode_back(cotangent)
        returned = with_halo(
            jnp.concatenate([g_left, g_right], axis=0).astype(jnp.bfloat16),
            (("region", 0),),
            halo_rows,
        ).astype(jnp.float32)
        g_buffer = jnp.concatenate([returned[:halo_rows], returned[-halo_rows:]], axis=0)
        g_mesh = g_mesh.at[send_rows].add(g_buffer)
        (g_encode,) = encode_back((g_mesh, g_grid))
        summed = jax.tree.map(jnp.add, g_params, g_encode)
        totals = summed if totals is None else jax.tree.map(jnp.add, totals, summed)
        loss_local = loss_local + loss_part
    reduced = (
        lax.psum_scatter(totals[0], "row", scatter_dimension=1, tiled=True),
        lax.psum_scatter(totals[1], "row", scatter_dimension=1, tiled=True),
        lax.psum_scatter(totals[2], "row", scatter_dimension=0, tiled=True),
        lax.psum_scatter(totals[3], "row", scatter_dimension=1, tiled=True),
        lax.psum_scatter(totals[4], "row", scatter_dimension=1, tiled=True),
    )
    reduced = lax.psum(reduced, "region")
    loss_sum = lax.psum(loss_local, ("region", "row"))
    g_matrices, g_in, g_out, g_gains, g_dates = reduced
    new_momentum = MUON_MOMENTUM * matrices_momentum + g_matrices
    squares = lax.psum(jnp.sum(new_momentum * new_momentum, axis=(1, 2)), "row")
    current = new_momentum * lax.rsqrt(squares + 1e-07)[:, None, None]
    gram_matrix = gram_sum(current)
    for sweep_index in range(NS_ITERS):
        if sweep_index > 0:
            gram_matrix = gram_sum(current)
        current = sweep_step(current, gram_matrix)
    new_matrices = matrices * (1.0 - MUON_RATE * WEIGHT_DECAY) - MUON_RATE * current
    new_in = adam_update(in_proj, g_in, in_first, in_second, MATRIX_RATE, WEIGHT_DECAY)
    new_out = adam_update(out_proj, g_out, out_first, out_second, MATRIX_RATE, WEIGHT_DECAY)
    new_gain = adam_update(norm_gains, g_gains, gains_first, gains_second, VECTOR_RATE, 0.0)
    new_date = adam_update(date_table, g_dates, date_first, date_second, VECTOR_RATE, 0.0)
    return (
        new_matrices,
        new_momentum,
        new_in[0],
        new_in[1],
        new_in[2],
        new_out[0],
        new_out[1],
        new_out[2],
        new_gain[0],
        new_gain[1],
        new_gain[2],
        new_date[0],
        new_date[1],
        new_date[2],
        loss_sum,
        valid_count,
    )


def solution(mesh):
    in_specs = (
        P("row", "region", None),
        P("row", "region", None),
        P("row", "region"),
        P(),
        P("region", None),
        P("region", None),
        P("region"),
        P("region", None),
        P("row"),
        P(None, "row", None),
        P(None, "row", None),
        P(None, "row"),
        P(None, "row"),
        P(None, "row"),
        P("row", None),
        P("row", None),
        P("row", None),
        P(None, "row"),
        P(None, "row"),
        P(None, "row"),
        P(None, "row"),
        P(None, "row"),
        P(None, "row"),
    )
    out_specs = (
        P(None, "row", None),
        P(None, "row", None),
        P(None, "row"),
        P(None, "row"),
        P(None, "row"),
        P("row", None),
        P("row", None),
        P("row", None),
        P(None, "row"),
        P(None, "row"),
        P(None, "row"),
        P(None, "row"),
        P(None, "row"),
        P(None, "row"),
        P(),
        P(),
    )
    return jax.shard_map(body, mesh=mesh, in_specs=in_specs, out_specs=out_specs, check_vma=False)
```

profile of v0, /device:TPU:0, one launch (start us, length us, event | category | flops | bytes accessed | tf_op | source)
XLA Modules:
  0.0 1872.1 jit_solution(10621190410980401170)
XLA Ops:
  16.5 13.7 all_gather.11
  37.1 16.9 all_gather.10
  58.0 11.7 gather_fusion
  84.4 11.7 gather_fusion.4
  110.6 11.7 gather_fusion.8
  133.9 9.2 all_gather.13
  143.1 13.3 all_gather.14
  185.2 10.8 collective-permute-start
  212.9 16.7 gather_fusion.6
  241.6 16.8 gather_fusion.10
  271.3 16.7 gather_fusion.2
  301.6 24.7 %gather_fusion.3 = f32[6144,512]{1,0:T(8,128)} fusion(f32[512,512]{1,0:T(8,128)S(1)} %copy.127, s32[6144]{0:T(1024)S(1)} %broadcast_clamp_fusion), kind=kCustom, calls=%fused_computation.3 | custom fusion | bytes 25190400 | tf_op jit(solution)/shard_map/jvp()/gather | solution.py:87
  326.4 19.2 %reshape.375 = f32[2048,3,512]{2,1,0:T(4,128)} reshape(f32[6144,512]{1,0:T(8,128)} %gather_fusion.3) | data formatting | bytes 25165824 | tf_op jit(solution)/shard_map/jvp()/gather | solution.py:87
  345.6 16.1 reduce_sum.580
  383.9 24.7 %gather_fusion.11 = f32[6144,512]{1,0:T(8,128)} fusion(f32[512,512]{1,0:T(8,128)S(1)} %copy.143, s32[6144]{0:T(1024)S(1)} %broadcast_clamp_fusion), kind=kCustom, calls=%fused_computation.11 | custom fusion | bytes 25190400 | tf_op jit(solution)/shard_map/jvp()/gather | solution.py:87
  408.7 19.2 %reshape.439 = f32[2048,3,512]{2,1,0:T(4,128)} reshape(f32[6144,512]{1,0:T(8,128)} %gather_fusion.11) | data formatting | bytes 25165824 | tf_op jit(solution)/shard_map/jvp()/gather | solution.py:87
  427.9 16.1 reduce_sum.637
  465.6 24.7 %gather_fusion.7 = f32[6144,512]{1,0:T(8,128)} fusion(f32[512,512]{1,0:T(8,128)S(1)} %copy-done, s32[6144]{0:T(1024)S(1)} %broadcast_clamp_fusion), kind=kCustom, calls=%fused_computation.7 | custom fusion | bytes 25190400 | tf_op jit(solution)/shard_map/jvp()/gather | solution.py:87
  490.3 19.2 %reshape.407 = f32[2048,3,512]{2,1,0:T(4,128)} reshape(f32[6144,512]{1,0:T(8,128)} %gather_fusion.7) | data formatting | bytes 25165824 | tf_op jit(solution)/shard_map/jvp()/gather | solution.py:87
  509.6 16.1 reduce_sum.609
  566.4 38.1 %all-reduce.30 = (f32[]{:T(128)}, f32[]{:T(128)}) all-reduce(f32[]{:T(128)} %convert_reduce_fusion, f32[]{:T(128)S(6)} %add.664), channel_id=1, replica_groups=mesh['region'=8,'row'=4] {'region','row'}, use_global_device_ids=true, to_apply=%region_10.11 | all-reduce | flops 2 | bytes 16 | tf_op jit(solution)/shard_map/psum | solution.py:155
  605.3 9.9 fusion.71
  621.3 10.8 multiply_reduce_fusion.2
  632.2 11.7 fusion.366
  645.9 9.4 fusion.133
  670.1 9.6 fusion.130
  693.1 9.5 fusion.127
  727.3 19.7 %reshape.446 = f32[6144,512]{1,0:T(8,128)} reshape(f32[2048,3,512]{2,1,0:T(4,128)} %broadcast_in_dim.218) | data formatting | bytes 25165824 | tf_op jit(solution)/shard_map/transpose(jvp())/broadcast_in_dim | solution.py:87
  747.0 37.4 %scatter_custom_fusion = f32[512,512]{1,0:T(8,128)S(1)} fusion(s32[6144]{0:T(1024)} %copy-done.132, f32[6144,512]{1,0:T(8,128)} %reshape.446, f32[]{:T(128)} %constant.147.clone.1), kind=kCustom, calls=%fused_computation.402 | custom fusion | flops 3145728 | bytes 1049088 | tf_op jit(solution)/shard_map/transpose(jvp())/scatter-add | solution.py:87
  799.1 19.7 %reshape.470 = f32[6144,512]{1,0:T(8,128)} reshape(f32[2048,3,512]{2,1,0:T(4,128)} %broadcast_in_dim.233) | data formatting | bytes 25165824 | tf_op jit(solution)/shard_map/transpose(jvp())/broadcast_in_dim | solution.py:87
  818.9 37.4 %scatter_custom_fusion.3 = f32[512,512]{1,0:T(8,128)S(1)} fusion(s32[6144]{0:T(1024)} %copy-done.132, f32[6144,512]{1,0:T(8,128)} %reshape.470, f32[]{:T(128)} %constant.147.clone.1), kind=kCustom, calls=%fused_computation.400 | custom fusion | flops 3145728 | bytes 1049088 | tf_op jit(solution)/shard_map/transpose(jvp())/scatter-add | solution.py:87
  870.7 19.9 %reshape.494 = f32[6144,512]{1,0:T(8,128)} reshape(f32[2048,3,512]{2,1,0:T(4,128)} %broadcast_in_dim.248) | data formatting | bytes 25165824 | tf_op jit(solution)/shard_map/transpose(jvp())/broadcast_in_dim | solution.py:87
  890.6 38.3 %scatter_custom_fusion.6 = f32[512,512]{1,0:T(8,128)} fusion(s32[6144]{0:T(1024)} %copy-done.132, f32[6144,512]{1,0:T(8,128)} %reshape.494, f32[]{:T(128)} %constant.147.clone.1), kind=kCustom, calls=%fused_computation.398 | custom fusion | flops 3145728 | bytes 1049088 | tf_op jit(solution)/shard_map/transpose(jvp())/scatter-add | solution.py:87
  953.8 29.0 %scatter_custom_fusion.7 = f32[640,512]{1,0:T(8,128)S(1)} fusion(s32[4096]{0:T(1024)} %copy-done.144, f32[4096,512]{1,0:T(8,128)} %gather_fusion.10, f32[512,512]{1,0:T(8,128)} %copy-done.73, f32[512,512]{1,0:T(8,128)S(1)} %copy-done.40, f32[]{:T(128)} %constant.149.clone.1, f32[]{:T(128)} %constant.147.clone.1), kind=kCustom, calls=%fused_computation.39 | custom fusion | flops 23068672 | bytes 11797504 | tf_op jit(solution)/shard_map/transpose(jvp())/scatter-add | solution.py:83
  1000.7 29.7 %scatter_custom_fusion.4 = f32[640,512]{1,0:T(8,128)} fusion(s32[4096]{0:T(1024)} %copy-done.144, f32[4096,512]{1,0:T(8,128)} %gather_fusion.6, f32[512,512]{1,0:T(8,128)S(1)} %convolution_multiply_fusion.4, f32[512,512]{1,0:T(8,128)S(1)} %copy-done.39, f32[]{:T(128)} %constant.149.clone.1, f32[]{:T(128)} %constant.147.clone.1), kind=kCustom, calls=%fused_computation.42 | custom fusion | flops 23068672 | bytes 11797504 | tf_op jit(solution)/shard_map/transpose(jvp())/scatter-add | solution.py:83
  1056.0 29.7 %scatter_custom_fusion.1 = f32[640,512]{1,0:T(8,128)} fusion(s32[4096]{0:T(1024)} %copy-done.144, f32[4096,512]{1,0:T(8,128)} %gather_fusion.2, f32[512,512]{1,0:T(8,128)S(1)} %convolution_multiply_fusion.5, f32[]{:T(128)} %constant.149.clone.1, f32[512,512]{1,0:T(8,128)S(1)} %copy-done.37, f32[]{:T(128)} %constant.147.clone.1), kind=kCustom, calls=%fused_computation.45 | custom fusion | flops 23068672 | bytes 11797504 | tf_op jit(solution)/shard_map/transpose(jvp())/scatter-add | solution.py:83
  1216.0 17.3 scatter_fusion
  1245.9 17.6 scatter_fusion.1
  1271.6 17.5 scatter_fusion.2
  1300.8 11.4 add_add_fusion
  1312.3 9.6 reduce-scatter.10.cloned.1.call-done
  1321.9 128.4 %reduce-scatter.8.cloned.1.call-done = f32[7,128,512]{2,1,0:T(8,128)} async-done(((f32[7,512,512]{2,1,0:T(8,128)}), f32[7,128,512]{2,1,0:T(8,128)}) %reduce-scatter.8.cloned.1.call-update) | async-done | bytes 1835024 | tf_op jit(solution)/shard_map/reduce_scatter | solution.py:197
  1450.4 65.7 %all-reduce.41.cloned.1.call-done = (f32[7,128,512]{2,1,0:T(8,128)}, f32[227,128]{1,0:T(8,128)}, f32[128,227]{0,1:T(8,128)}) async-done(((f32[7,128,512]{2,1,0:T(8,128)}, f32[227,128]{1,0:T(8,128)}, f32[128,227]{0,1:T(8,128)}), (f32[7,128,512]{2,1,0:T(8,128)}, f32[227,128]{1,0:T(8,128)}, f32[128,227]{0,1:T(8,128)})) %all-reduce.41.cloned.1.call-update) | async-done | bytes 2067472 | tf_op jit(solution)/shard_map/psum | solution.py:203
  1518.6 11.7 psum.72
  1548.0 125.0 %all-reduce.37.cloned.1.call-done = bf16[7,512,512]{2,1,0:T(8,128)(2,1)} async-done(((bf16[7,512,512]{2,1,0:T(8,128)(2,1)}), bf16[7,512,512]{2,1,0:T(8,128)(2,1)}) %all-reduce.37.cloned.1.call-update) | async-done | bytes 3670032 | tf_op jit(solution)/shard_map/psum | solution.py:106
  1695.4 19.2 %reduce-scatter.14.cloned.1.call-done = f32[8,128]{1,0:T(8,128)} async-done(((f32[8,512]{1,0:T(8,128)}), f32[8,128]{1,0:T(8,128)}) %reduce-scatter.14.cloned.1.call-update) | async-done | bytes 4112 | tf_op jit(solution)/shard_map/reduce_scatter | solution.py:201
  1714.6 12.5 all-reduce.31
  1729.9 123.3 %all-reduce.39.cloned.1.call-done = bf16[7,512,512]{2,1,0:T(8,128)(2,1)} async-done(((bf16[7,512,512]{2,1,0:T(8,128)(2,1)}), bf16[7,512,512]{2,1,0:T(8,128)(2,1)}) %all-reduce.39.cloned.1.call-update) | async-done | bytes 3670032 | tf_op jit(solution)/shard_map/psum | solution.py:106
  (727 shorter events, 597.4 us)
Async XLA Ops:
  7.2 151.6 %all-gather.2.cloned.1.call-start = ((), (), s32[]{:S(2)}) async-start(), calls=%async_computation.5 | async-start | bytes 4587520 | tf_op jit(solution)/shard_map/all_gather | solution.py:96
  9.8 1302.5 %reduce-scatter.12.cloned.1.call-start = ((), (), s32[]{:S(2)}) async-start(), calls=%async_computation.10 | async-start | bytes 593920 | tf_op jit(solution)/shard_map/reduce_scatter | solution.py:199
  33.7 124.4 %copy-start.144 = (s32[4096]{0:T(1024)}, s32[4096]{0:T(1024)S(1)}, u32[]{:S(2)}) copy-start(s32[4096]{0:T(1024)S(1)} %reshape.364) | copy-start | bytes 49156
  35.2 123.0 %copy-start.132 = (s32[6144]{0:T(1024)}, s32[6144]{0:T(1024)S(1)}, u32[]{:S(2)}) copy-start(s32[6144]{0:T(1024)S(1)} %reshape.372) | copy-start | bytes 73732
  80.0 78.8 %copy-start.41 = (f32[512,512]{0,1:T(8,128)}, f32[512,512]{0,1:T(8,128)S(1)}, u32[]{:S(2)}) copy-start(f32[512,512]{0,1:T(8,128)S(1)} %copy.122) | copy-start | bytes 3145732
  106.3 57.6 %copy-start.44 = (f32[512,512]{0,1:T(8,128)}, f32[512,512]{0,1:T(8,128)S(1)}, u32[]{:S(2)}) copy-start(f32[512,512]{0,1:T(8,128)S(1)} %copy.132) | copy-start | bytes 3145732
  158.1 139.8 %copy-start.169 = (f32[1,512]{1,0:T(1,128)}, f32[1,512]{1,0:T(1,128)S(1)}, u32[]{:S(2)}) copy-start(f32[1,512]{1,0:T(1,128)S(1)} %get-tuple-element.107) | copy-start | bytes 6148
  174.8 31.1 %collective-permute-start.4 = (bf16[64,512]{0,1:T(8,128)(2,1)}, bf16[64,512]{0,1:T(8,128)(2,1)}, u32[]{:S(2)}, u32[]{:S(2)}) collective-permute-start(bf16[64,512]{0,1:T(8,128)(2,1)} %get-tuple-element.94), channel_id=1, source_target_pairs={{0,4},{4,8},{8,12},{12,16},{16,20},{20,24},{24,28},{28,0},{1,5},{5... | collective-permute-start | bytes 196616 | tf_op jit(solution)/shard_map/ppermute | solution.py:29
  174.8 34.6 %collective-permute-start.5 = (bf16[64,512]{0,1:T(8,128)(2,1)}, bf16[64,512]{0,1:T(8,128)(2,1)}, u32[]{:S(2)}, u32[]{:S(2)}) collective-permute-start(bf16[64,512]{0,1:T(8,128)(2,1)} %get-tuple-element.95), channel_id=1, source_target_pairs={{4,0},{8,4},{12,8},{16,12},{20,16},{24,20},{28,24},{0,28},{5,1},{9... | collective-permute-start | bytes 196616 | tf_op jit(solution)/shard_map/ppermute | solution.py:32
  180.6 58.3 %collective-permute-start.8 = (bf16[64,512]{0,1:T(8,128)(2,1)}, bf16[64,512]{0,1:T(8,128)(2,1)S(1)}, u32[]{:S(2)}, u32[]{:S(2)}) collective-permute-start(bf16[64,512]{0,1:T(8,128)(2,1)} %get-tuple-element.98), channel_id=1, source_target_pairs={{0,4},{4,8},{8,12},{12,16},{16,20},{20,24},{24,28},{28,0},{1,5},{5... | collective-permute-start | bytes 196616 | tf_op jit(solution)/shard_map/ppermute | solution.py:29
  180.6 58.3 %collective-permute-start.9 = (bf16[64,512]{0,1:T(8,128)(2,1)}, bf16[64,512]{0,1:T(8,128)(2,1)S(1)}, u32[]{:S(2)}, u32[]{:S(2)}) collective-permute-start(bf16[64,512]{0,1:T(8,128)(2,1)} %get-tuple-element.99), channel_id=1, source_target_pairs={{4,0},{8,4},{12,8},{16,12},{20,16},{24,20},{28,24},{0,28},{5,1},{9... | collective-permute-start | bytes 196616 | tf_op jit(solution)/shard_map/ppermute | solution.py:32
  185.2 82.4 %collective-permute-start = (bf16[64,512]{0,1:T(8,128)(2,1)}, bf16[64,512]{0,1:T(8,128)(2,1)S(1)}, u32[]{:S(2)}, u32[]{:S(2)}) collective-permute-start(bf16[64,512]{0,1:T(8,128)(2,1)} %get-tuple-element.96), channel_id=1, source_target_pairs={{0,4},{4,8},{8,12},{12,16},{16,20},{20,24},{24,28},{28,0},{1,5},{5... | collective-permute-start | bytes 196616 | tf_op jit(solution)/shard_map/ppermute | solution.py:29
  205.8 61.8 %collective-permute-start.1 = (bf16[64,512]{0,1:T(8,128)(2,1)}, bf16[64,512]{0,1:T(8,128)(2,1)}, u32[]{:S(2)}, u32[]{:S(2)}) collective-permute-start(bf16[64,512]{0,1:T(8,128)(2,1)} %get-tuple-element.97), channel_id=1, source_target_pairs={{4,0},{8,4},{12,8},{16,12},{20,16},{24,20},{28,24},{0,28},{5,1},{9... | collective-permute-start | bytes 196616 | tf_op jit(solution)/shard_map/ppermute | solution.py:32
  238.6 59.3 %copy-start.22 = (f32[512,512]{0,1:T(8,128)}, f32[512,512]{0,1:T(8,128)S(1)}, u32[]{:S(2)}) copy-start(f32[512,512]{0,1:T(8,128)S(1)} %get-tuple-element.150) | copy-start | bytes 3145732
  238.7 59.3 %copy-start.153 = (f32[512]{0:T(512)}, f32[512]{0:T(512)S(1)}, u32[]{:S(2)}) copy-start(f32[512]{0:T(512)S(1)} %broadcast_multiply_fusion.5) | copy-start | bytes 6148
  238.9 59.1 %copy-start.171 = (f32[512]{0:T(512)}, f32[512]{0:T(512)S(1)}, u32[]{:S(2)}) copy-start(f32[512]{0:T(512)S(1)} %fusion.317) | copy-start | bytes 6148
  457.2 175.0 %copy-start.124 = (f32[2048]{0:T(1024)}, f32[2048]{0:T(1024)S(1)}, u32[]{:S(2)}) copy-start(f32[2048]{0:T(1024)S(1)} %broadcast_multiply_fusion) | copy-start | bytes 24580
  465.6 166.6 %copy-start.140 = (f32[2048]{0:T(1024)}, f32[2048]{0:T(1024)S(1)}, u32[]{:S(2)}) copy-start(f32[2048]{0:T(1024)S(1)} %fusion.311) | copy-start | bytes 24580
  870.6 60.9 %copy-start.23 = (f32[512,512]{0,1:T(8,128)S(1)}, f32[512,512]{0,1:T(8,128)}, u32[]{:S(2)}) copy-start(f32[512,512]{0,1:T(8,128)} %copy-done.22) | copy-start | bytes 3145732
  870.6 60.9 %copy-start.26 = (f32[512,512]{0,1:T(8,128)S(1)}, f32[512,512]{0,1:T(8,128)}, u32[]{:S(2)}) copy-start(f32[512,512]{0,1:T(8,128)} %copy-done.24) | copy-start | bytes 3145732
  870.6 60.9 %copy-start.28 = (f32[512,512]{0,1:T(8,128)S(1)}, f32[512,512]{0,1:T(8,128)}, u32[]{:S(2)}) copy-start(f32[512,512]{0,1:T(8,128)} %copy-done.27) | copy-start | bytes 3145732
  870.6 60.9 %copy-start.154 = (f32[512]{0:T(512)S(1)}, f32[512]{0:T(512)}, u32[]{:S(2)}) copy-start(f32[512]{0:T(512)} %copy-done.153) | copy-start | bytes 6148
  870.6 60.9 %copy-start.156 = (f32[512]{0:T(512)S(1)}, f32[512]{0:T(512)}, u32[]{:S(2)}) copy-start(f32[512]{0:T(512)} %copy-done.155) | copy-start | bytes 6148
  870.6 60.9 %copy-start.158 = (f32[512]{0:T(512)S(1)}, f32[512]{0:T(512)}, u32[]{:S(2)}) copy-start(f32[512]{0:T(512)} %copy-done.157) | copy-start | bytes 6148
  870.6 60.9 %copy-start.170 = (f32[1,512]{1,0:T(1,128)S(1)}, f32[1,512]{1,0:T(1,128)}, u32[]{:S(2)}) copy-start(f32[1,512]{1,0:T(1,128)} %copy-done.169) | copy-start | bytes 6148
  870.6 60.9 %copy-start.172 = (f32[512]{0:T(512)S(1)}, f32[512]{0:T(512)}, u32[]{:S(2)}) copy-start(f32[512]{0:T(512)} %copy-done.171) | copy-start | bytes 6148
  870.7 60.9 %copy-start.174 = (f32[512]{0:T(512)S(1)}, f32[512]{0:T(512)}, u32[]{:S(2)}) copy-start(f32[512]{0:T(512)} %copy-done.173) | copy-start | bytes 6148
  870.7 60.9 %copy-start.176 = (f32[512]{0:T(512)S(1)}, f32[512]{0:T(512)}, u32[]{:S(2)}) copy-start(f32[512]{0:T(512)} %copy-done.175) | copy-start | bytes 6148
  1110.2 211.7 %reduce-scatter.10.cloned.1.call-start = ((), (), s32[]{:S(2)}) async-start(), calls=%async_computation.9 | async-start | bytes 593920 | tf_op jit(solution)/shard_map/reduce_scatter | solution.py:198
  1119.6 16.6 collective-permute-start.10
  1119.7 19.2 %collective-permute-start.11 = (bf16[64,512]{1,0:T(8,128)(2,1)S(1)}, bf16[64,512]{1,0:T(8,128)(2,1)S(1)}, u32[]{:S(2)}, u32[]{:S(2)}) collective-permute-start(bf16[64,512]{1,0:T(8,128)(2,1)S(1)} %get-tuple-element.87), channel_id=1, source_target_pairs={{4,0},{8,4},{12,8},{16,12},{20,16},{24,20},{28,24},{0,28},{5,1},{9... | collective-permute-start | bytes 196616 | tf_op jit(solution)/shard_map/ppermute | solution.py:32
  1125.3 16.0 collective-permute-start.6
  1125.3 16.0 collective-permute-start.7
  1130.8 16.6 collective-permute-start.2
  1136.3 11.2 collective-permute-start.3
  1300.7 149.7 %reduce-scatter.8.cloned.1.call-start = ((), (), s32[]{:S(2)}) async-start(), calls=%async_computation.6 | async-start | bytes 9175040 | tf_op jit(solution)/shard_map/reduce_scatter | solution.py:197
  1312.3 203.9 %all-reduce.41.cloned.1.call-start = ((), (), s32[]{:S(2)}) async-start(), calls=%async_computation.13 | async-start | bytes 4145152 | tf_op jit(solution)/shard_map/psum | solution.py:203
  1450.4 222.6 %all-reduce.37.cloned.1.call-start = ((), (), s32[]{:S(2)}) async-start(), calls=%async_computation.7 | async-start | bytes 7340032 | tf_op jit(solution)/shard_map/psum | solution.py:106
  1538.2 156.3 %reduce-scatter.16.cloned.1.call-start = ((), (), s32[]{:S(2)}) async-start(), calls=%async_computation.12 | async-start | bytes 327680
  1547.2 167.4 %reduce-scatter.14.cloned.1.call-start = ((), (), s32[]{:S(2)}) async-start(), calls=%async_computation.11 | async-start | bytes 20480 | tf_op jit(solution)/shard_map/reduce_scatter | solution.py:201
  1548.0 305.3 %all-reduce.39.cloned.1.call-start = ((), (), s32[]{:S(2)}) async-start(), calls=%async_computation.8 | async-start | bytes 7340032 | tf_op jit(solution)/shard_map/psum | solution.py:106
  1685.7 42.6 %copy-start.120 = (f32[227,128]{1,0:T(8,128)S(1)}, f32[227,128]{1,0:T(8,128)}, u32[]{:S(2)}) copy-start(f32[227,128]{1,0:T(8,128)} %param.34) | copy-start | bytes 348676
  1685.7 42.6 %copy-start.126 = (f32[227,128]{1,0:T(8,128)S(1)}, f32[227,128]{1,0:T(8,128)}, u32[]{:S(2)}) copy-start(f32[227,128]{1,0:T(8,128)} %param.35) | copy-start | bytes 348676
  1685.8 42.6 %copy-start.127 = (f32[227,128]{1,0:T(8,128)S(1)}, f32[227,128]{1,0:T(8,128)}, u32[]{:S(2)}) copy-start(f32[227,128]{1,0:T(8,128)} %param.36) | copy-start | bytes 348676
  1685.8 43.4 %copy-start.121 = (f32[128,227]{0,1:T(8,128)S(1)}, f32[128,227]{0,1:T(8,128)}, u32[]{:S(2)}) copy-start(f32[128,227]{0,1:T(8,128)} %param.37) | copy-start | bytes 348676
  1685.8 43.3 %copy-start.128 = (f32[128,227]{0,1:T(8,128)S(1)}, f32[128,227]{0,1:T(8,128)}, u32[]{:S(2)}) copy-start(f32[128,227]{0,1:T(8,128)} %param.38) | copy-start | bytes 348676
  1685.8 43.3 %copy-start.129 = (f32[128,227]{0,1:T(8,128)S(1)}, f32[128,227]{0,1:T(8,128)}, u32[]{:S(2)}) copy-start(f32[128,227]{0,1:T(8,128)} %param.39) | copy-start | bytes 348676
  1685.8 43.3 %copy-start.130 = (f32[128,227]{0,1:T(8,128)S(1)}, f32[128,227]{0,1:T(8,128)}, u32[]{:S(2)}) copy-start(f32[128,227]{0,1:T(8,128)} %get-tuple-element.43) | copy-start | bytes 348676
  (193 other events, 1872.6 us)
Sparse Core Ops, SparseCore 0:
  10.2 78.6 all-gather.1
  1110.3 22.1 reduce-scatter.11
  1300.8 21.0 reduce-scatter.9
  1324.1 126.2 reduce-scatter.7
  1453.8 62.3 all-reduce.40
  1538.3 134.6 all-reduce.36
  1675.8 18.6 reduce-scatter.15
  1697.4 17.1 reduce-scatter.13
  1717.0 136.2 all-reduce.38
where the time goes:
time: 1890 us; the launch traced here: 1870 us
  waiting for transfers between devices  473 us (25%)
  other arithmetic  445 us (24%)
  local copies, waits for them, and re-layouts  398 us (21%)
  matrix products  387 us (20%)
  blocking collectives  115 us (6%)
  starting transfers between devices  27.1 us (1%)
  between operations  26.1 us (1%)
    dot_general x78, matrix products, product(): return jnp.dot(left_side, right_side, precision=HIGHEST)  347 us
    psum x2, waiting for transfers between devices, gram_sum(): lax.psum(jnp.einsum('mrk,mrl->mkl', block, block, precision=HIGHEST).asty...  248 us
    gather x6, local copies, waits for them, and re-layouts, decode(): decoded = jnp.mean(mesh_two[mesh_to_grid], axis=1)  132 us
    reduce_scatter x1, waiting for transfers between devices, body(): lax.psum_scatter(totals[0], 'row', scatter_dimension=1, tiled=True)  128 us
    scatter-add x3, other arithmetic, decode(): decoded = jnp.mean(mesh_two[mesh_to_grid], axis=1)  113 us
    scatter-add x3, other arithmetic, decode(): pre_act = senders[mesh_edges] + receivers[:, None, :]  88.4 us
    broadcast_in_dim x7, local copies, waits for them, and re-layouts, decode(): decoded = jnp.mean(mesh_two[mesh_to_grid], axis=1)  82.7 us
    psum x1, waiting for transfers between devices, body(): reduced = lax.psum(reduced, 'region')  65.7 us
  transfers between devices with their start and end apart: 21, of which 7 were waited for; matrix products, arithmetic and copies ran while one was open for 21% of the time, Pallas kernels for 0%

commit v1 on v0

v1 whole, which is shorter than its diff:
```python
from functools import partial

import jax
import jax.numpy as jnp
from jax import lax
from jax.experimental import pallas as pl
from jax.experimental.pallas import tpu as pltpu
from jax.sharding import PartitionSpec as P

NS_ITERS = 2
STEP = 10
NS_COEFFS = (3.4445, -4.775, 2.0315)
MUON_RATE = 0.8
MUON_MOMENTUM = 0.95
MATRIX_RATE = 0.05
VECTOR_RATE = 0.2
BETA_ONE = 0.9
BETA_TWO = 0.95
WEIGHT_DECAY = 0.01

F32 = jnp.float32
BF16 = jnp.bfloat16
HIGHEST = lax.Precision.HIGHEST
LATENT = 512
BLOCK = 512
T_TYPE = F32
VMEM_BYTES = 60 * 1024 * 1024


def dot(left, right):
    return jnp.dot(left, right, preferred_element_type=F32)


def dot_nt(left, right):
    return lax.dot_general(left, right, (((1,), (1,)), ((), ())), preferred_element_type=F32)


def dot_tn(left, right):
    return lax.dot_general(left, right, (((0,), (0,)), ((), ())), preferred_element_type=F32)


def split_two(values):
    high = values.astype(BF16)
    return high, (values - high.astype(F32)).astype(BF16)


def sigmoid(values):
    return 0.5 * jnp.tanh(0.5 * values) + 0.5


def normalise(values):
    centred = values - jnp.mean(values, axis=-1, keepdims=True)
    spread = jnp.mean(centred * centred, axis=-1, keepdims=True)
    scale = lax.rsqrt(spread + 1e-05)
    return centred * scale, scale


def norm_back(grad, gain, unit, scale):
    scaled = gain * grad
    mean_one = jnp.mean(scaled, axis=-1, keepdims=True)
    mean_two = jnp.mean(scaled * unit, axis=-1, keepdims=True)
    return scale * (scaled - mean_one - unit * mean_two)


def count_columns(index, width, count):
    lanes = lax.broadcasted_iota(jnp.int32, (index.shape[0], width), 1)
    total = None
    for k in range(count):
        one = jnp.where(lanes == index[:, k : k + 1], 1.0, 0.0)
        total = one if total is None else total + one
    return total.astype(BF16)


def columns_of(index):
    short = 8 - index.shape[0]
    if short > 0:
        index = jnp.concatenate([index, jnp.zeros((short, index.shape[1]), index.dtype)], axis=0)
    return jnp.transpose(index)


def count_rows(index, height):
    lines = lax.broadcasted_iota(jnp.int32, (height, index.shape[1]), 0)
    total = None
    for k in range(index.shape[0]):
        one = jnp.where(lines == index[k : k + 1, :], 1.0, 0.0)
        total = one if total is None else total + one
    return total.astype(BF16)


def encode_kernel(
    day_ref, x_ref, picks_ref, win_ref, m0_ref, m1_ref, gains_ref, date_ref, send_ref,
    x4_ref, a0_ref, h1_ref, t1_ref, unit_ref, scale_ref, mesh_ref, sent_ref, buf_ref,
    pick_ref, out_ref,
):
    @pl.when(pl.program_id(0) == 0)
    def _():
        count = picks_ref.shape[0]
        pick_ref[...] = count_columns(columns_of(picks_ref[...]), pick_ref.shape[1], count)
        out_ref[...] = count_columns(columns_of(send_ref[...]), out_ref.shape[1], 1)

    x4 = dot_nt(pick_ref[...], x_ref[0]) * (1.0 / picks_ref.shape[0])
    high, low = split_two(x4)
    win = win_ref[...]
    agg = dot(high, win) + dot(low, win) + date_ref[pl.ds(day_ref[pl.program_id(0)], 1), :]
    a0 = agg.astype(BF16)
    pre = dot(a0, m0_ref[...])
    gate = sigmoid(pre)
    hid = pre * gate
    h1 = hid.astype(BF16)
    unit, scale = normalise(dot(h1, m1_ref[...]))
    mesh = agg + unit * gains_ref[0:1, :]
    sent = mesh.astype(BF16)
    x4_ref[0] = high
    a0_ref[0] = a0
    h1_ref[0] = h1
    t1_ref[0] = gate + hid * (1.0 - gate)
    unit_ref[0] = unit
    scale_ref[0] = scale
    mesh_ref[0] = mesh
    sent_ref[0] = sent
    buf_ref[0] = dot(out_ref[...], sent).astype(BF16)


def main_kernel(
    count_ref, day_ref, mesh_ref, sent_ref, left_ref, right_ref, x_ref, y_ref, valid_ref, varw_ref,
    date_ref, edge_ref, pick_row_ref,
    win_ref, wout_ref, m2_ref, m3_ref, m4_ref, m5_ref, m6_ref, gains_ref,
    gm_ref, gout_ref, gxd_ref, dsum_ref, ggain_ref, loss_ref, dmesh_ref, dhalo_ref,
    eh_ref, eht_ref, d_ref, dt_ref, ext_ref, t_ref, mm_ref, acc_ref,
):
    nodes = mesh_ref.shape[1]
    table = ext_ref.shape[0]
    points = x_ref.shape[2]
    k_edge = edge_ref.shape[0]
    k_pick = pick_row_ref.shape[0]
    halo = left_ref.shape[1]

    @pl.when(pl.program_id(0) == 0)
    def _():
        edge_columns = columns_of(edge_ref[...])
        for k in range(k_edge):
            rows = slice(k * nodes, (k + 1) * nodes)
            eh_ref[rows, :] = count_columns(edge_columns[:, k : k + 1], table, 1)
            eht_ref[:, rows] = count_rows(edge_ref[k : k + 1, :], table)

        def build(i, carry):
            rows = pl.ds(pl.multiple_of(i * BLOCK, BLOCK), BLOCK)
            picks = pick_row_ref[:, rows]
            d_ref[rows, :] = count_columns(columns_of(picks), nodes, k_pick)
            dt_ref[:, rows] = count_rows(picks, nodes)
            return carry

        lax.fori_loop(0, points // BLOCK, build, 0)
        gm_ref[...] = jnp.zeros_like(gm_ref)
        gout_ref[...] = jnp.zeros_like(gout_ref)
        gxd_ref[...] = jnp.zeros_like(gxd_ref)
        ggain_ref[...] = jnp.zeros_like(ggain_ref)
        loss_ref[...] = jnp.zeros_like(loss_ref)

    sent = sent_ref[0]
    ext_ref[:nodes, :] = sent
    ext_ref[nodes : nodes + halo, :] = left_ref[0]
    ext_ref[nodes + halo :, :] = right_ref[0]
    receivers = dot(sent, m3_ref[...])

    def edge(k, carry):
        hid_sum, t_sum = carry
        rows = pl.ds(pl.multiple_of(k * nodes, nodes), nodes)
        picked = dot(eh_ref[rows, :], ext_ref[...]).astype(BF16)
        pre = dot(picked, m2_ref[...]) + receivers
        gate = sigmoid(pre)
        hid = pre * gate
        t = gate + hid * (1.0 - gate)
        t_ref[rows, :] = t.astype(t_ref.dtype)
        return hid_sum + hid.astype(BF16).astype(F32), t_sum + t

    zero = jnp.zeros((nodes, LATENT), F32)
    hid_sum, t_sum = lax.fori_loop(0, k_edge, edge, (zero, zero))
    h_high, h_low = split_two(hid_sum * (1.0 / k_edge))
    m4 = m4_ref[...]
    unit2, scale2 = normalise(dot(h_high, m4) + dot(h_low, m4))
    mesh2 = mesh_ref[0] + unit2 * gains_ref[1:2, :]
    m_high, m_low = split_two(mesh2)
    mm_ref[:nodes, :] = m_high
    mm_ref[nodes:, :] = m_low

    acc_ref[...] = jnp.zeros_like(acc_ref)
    dsum_ref[...] = jnp.zeros_like(dsum_ref)
    member = pl.program_id(0)
    date = date_ref[pl.ds(day_ref[member], 1), :]
    gain3 = gains_ref[2:3, :]
    varw = varw_ref[...]

    def grid_block(i, carry):
        rows = pl.ds(pl.multiple_of(i * BLOCK, BLOCK), BLOCK)
        picks = d_ref[rows, :]
        dec = dot(picks, mm_ref[:nodes, :]) + dot(picks, mm_ref[nodes:, :])
        a2 = (dec * (1.0 / k_pick)).astype(BF16)
        pre = dot(a2, m5_ref[...])
        gate = sigmoid(pre)
        hid = pre * gate
        t = gate + hid * (1.0 - gate)
        h2 = hid.astype(BF16)
        unit, scale = normalise(dot(h2, m6_ref[...]))
        x = x_ref[0, :, rows]
        grid = dot_tn(x, win_ref[...]) + date + unit * gain3
        grid = grid.astype(BF16)
        misfit = x.astype(F32) + dot_nt(wout_ref[...], grid) - y_ref[0, :, rows].astype(F32)
        valid = valid_ref[pl.ds(member, 1), rows].astype(F32)
        weighted = valid * varw * misfit
        loss_ref[...] += jnp.sum(weighted * misfit, axis=1, keepdims=True)
        dp = weighted * count_ref[0]
        dsum_ref[0] += jnp.sum(dp, axis=1, keepdims=True)
        dp = dp.astype(BF16)
        gout_ref[...] += dot(dp, grid)
        gxd_ref[...] += dot_nt(x, dp)
        dgrid = dot_tn(dp, wout_ref[...])
        ggain_ref[1:2, :] += jnp.sum(dgrid * unit, axis=0, keepdims=True)
        dc = norm_back(dgrid, gain3, unit, scale).astype(BF16)
        gm_ref[4] += dot_tn(h2, dc)
        du = (dot_nt(dc, m6_ref[...]) * t).astype(BF16)
        gm_ref[3] += dot_tn(a2, du)
        ddec = dot_nt(du, m5_ref[...]).astype(BF16)
        acc_ref[...] += dot(dt_ref[:, rows], ddec)
        return carry

    lax.fori_loop(0, points // BLOCK, grid_block, 0)

    dmesh2 = acc_ref[...] * (1.0 / k_pick)
    ggain_ref[0:1, :] += jnp.sum(dmesh2 * unit2, axis=0, keepdims=True)
    dagg = norm_back(dmesh2, gains_ref[1:2, :], unit2, scale2).astype(BF16)
    gm_ref[2] += dot_tn(h_high, dagg)
    dhid = dot_nt(dagg, m4_ref[...]) * (1.0 / k_edge)
    dr = (dhid * t_sum).astype(BF16)
    gm_ref[1] += dot_tn(sent, dr)

    def edge_back(k, total):
        rows = pl.ds(pl.multiple_of(k * nodes, nodes), nodes)
        dpre = (dhid * t_ref[rows, :].astype(F32)).astype(BF16)
        return total + dot(eht_ref[:, rows], dpre)

    ds = lax.fori_loop(0, k_edge, edge_back, jnp.zeros((table, LATENT), F32)).astype(BF16)
    gm_ref[0] += dot_tn(ext_ref[...], ds)
    dext = dot_nt(ds, m2_ref[...])
    dmesh_ref[0] = dmesh2 + dext[:nodes, :] + dot_nt(dr, m3_ref[...])
    dhalo_ref[0] = dext[nodes:, :].astype(BF16)


def encode_back_kernel(
    dmesh_ref, ret_ref, send_ref, x4_ref, a0_ref, h1_ref, t1_ref, unit_ref, scale_ref, m0_ref, m1_ref,
    gains_ref, wout_ref, gxd_ref, dsum_ref, gm_ref, gin_ref, ggain_ref, gdate_ref, back_ref,
):
    @pl.when(pl.program_id(0) == 0)
    def _():
        back_ref[...] = count_rows(send_ref[...], back_ref.shape[0])
        gm_ref[...] = jnp.zeros_like(gm_ref)
        ggain_ref[...] = jnp.zeros_like(ggain_ref)
        high, low = split_two(gxd_ref[...])
        wout = wout_ref[...]
        gin_ref[...] = dot(high, wout) + dot(low, wout)

    dmesh = dmesh_ref[0] + dot(back_ref[...], ret_ref[0])
    unit = unit_ref[0]
    ggain_ref[...] += jnp.sum(dmesh * unit, axis=0, keepdims=True)
    dc = norm_back(dmesh, gains_ref[0:1, :], unit, scale_ref[0]).astype(BF16)
    gm_ref[1] += dot_tn(h1_ref[0], dc)
    du = (dot_nt(dc, m1_ref[...]) * t1_ref[0]).astype(BF16)
    gm_ref[0] += dot_tn(a0_ref[0], du)
    dagg = dmesh + dot_nt(du, m0_ref[...])
    gin_ref[...] += dot_tn(x4_ref[0], dagg.astype(BF16))
    high, low = split_two(dsum_ref[0])
    wout = wout_ref[...]
    gdate_ref[0] = jnp.sum(dagg, axis=0, keepdims=True) + dot_tn(high, wout) + dot_tn(low, wout)


def whole(shape):
    return pl.BlockSpec(shape, lambda m: (0,) * len(shape))


def per_member(shape):
    return pl.BlockSpec((1,) + shape, lambda m: (m, 0, 0))


def call(kernel, members, in_specs, out_shapes, out_specs, scratch, cost):
    return pl.pallas_call(
        kernel,
        grid=(members,),
        in_specs=in_specs,
        out_shape=out_shapes,
        out_specs=out_specs,
        scratch_shapes=scratch,
        compiler_params=pltpu.CompilerParams(
            dimension_semantics=("arbitrary",), vmem_limit_bytes=VMEM_BYTES
        ),
        cost_estimate=pl.CostEstimate(flops=cost, bytes_accessed=32 << 20, transcendentals=0),
    )


def shape_of(shape, dtype):
    return jax.ShapeDtypeStruct(shape, dtype)


def cyclic(block, halo):
    count = lax.axis_size("region")
    forward = [(i, (i + 1) % count) for i in range(count)]
    backward = [(target, source) for source, target in forward]
    low = lax.ppermute(block[:, -halo:], "region", forward)
    high = lax.ppermute(block[:, :halo], "region", backward)
    return low, high


def gram_sum(block):
    return lax.psum(
        jnp.einsum("mrk,mrl->mkl", block, block, precision=HIGHEST).astype(BF16), "row"
    ).astype(F32)


def sweep_step(current, gram_matrix):
    square = jnp.einsum("mkj,mjl->mkl", gram_matrix, gram_matrix, precision=HIGHEST)
    mixing = NS_COEFFS[1] * gram_matrix + NS_COEFFS[2] * square
    return NS_COEFFS[0] * current + jnp.einsum("mrk,mkl->mrl", current, mixing, precision=HIGHEST)


def adam_update(weight, gradient, first_moment, second_moment, step_rate, decay_rate):
    first_new = BETA_ONE * first_moment + (1.0 - BETA_ONE) * gradient
    second_new = BETA_TWO * second_moment + (1.0 - BETA_TWO) * gradient * gradient
    unbiased_one = first_new / (1.0 - BETA_ONE**STEP)
    unbiased_two = second_new / (1.0 - BETA_TWO**STEP)
    weight_new = weight * (1.0 - step_rate * decay_rate) - step_rate * unbiased_one / (
        jnp.sqrt(unbiased_two) + 1e-08
    )
    return (weight_new, first_new, second_new)


def body(
    inputs,
    targets,
    valid_steps,
    var_weights,
    grid_to_mesh,
    mesh_edges,
    send_rows,
    mesh_to_grid,
    date_index,
    matrices,
    matrices_momentum,
    in_proj,
    in_first,
    in_second,
    out_proj,
    out_first,
    out_second,
    norm_gains,
    gains_first,
    gains_second,
    date_table,
    date_first,
    date_second,
):
    inputs = jnp.swapaxes(inputs, 1, 2)
    targets = jnp.swapaxes(targets, 1, 2)
    members, variables, points = inputs.shape
    nodes = grid_to_mesh.shape[0]
    halo = send_rows.shape[0] // 2
    table = nodes + 2 * halo
    k_edge = mesh_edges.shape[1]
    k_pick = mesh_to_grid.shape[1]
    dates = date_table.shape[0]

    masks = valid_steps.astype(F32)
    valid_count = lax.psum(jnp.sum(masks), ("region", "row"))
    full_m = lax.all_gather(matrices.astype(BF16), "row", axis=1, tiled=True)
    full_in = lax.all_gather(in_proj.astype(BF16), "row", axis=1, tiled=True)
    full_out = lax.all_gather(out_proj.T.astype(BF16), "row", axis=1, tiled=True)
    full_gains = lax.all_gather(norm_gains.astype(BF16), "row", axis=1, tiled=True).astype(F32)
    full_dates = lax.all_gather(date_table.astype(BF16), "row", axis=1, tiled=True).astype(F32)
    scalars = pl.BlockSpec(memory_space=pltpu.SMEM)

    node_block = per_member((nodes, LATENT))
    matrix = whole((LATENT, LATENT))
    x4, a0, h1, t1, unit1, scale1, mesh1, sent, buf = call(
        encode_kernel,
        members,
        [
            scalars,
            per_member((variables, points)),
            whole((grid_to_mesh.shape[1], nodes)),
            whole(full_in.shape),
            matrix,
            matrix,
            whole(full_gains.shape),
            whole(full_dates.shape),
            whole((1, 2 * halo)),
        ],
        [
            shape_of((members, nodes, variables), BF16),
            shape_of((members, nodes, LATENT), BF16),
            shape_of((members, nodes, LATENT), BF16),
            shape_of((members, nodes, LATENT), F32),
            shape_of((members, nodes, LATENT), F32),
            shape_of((members, nodes, 1), F32),
            shape_of((members, nodes, LATENT), F32),
            shape_of((members, nodes, LATENT), BF16),
            shape_of((members, 2 * halo, LATENT), BF16),
        ],
        [
            per_member((nodes, variables)),
            node_block,
            node_block,
            node_block,
            node_block,
            per_member((nodes, 1)),
            node_block,
            node_block,
            per_member((2 * halo, LATENT)),
        ],
        [pltpu.VMEM((nodes, points), BF16), pltpu.VMEM((2 * halo, nodes), BF16)],
        6_000_000_000,
    )(
        date_index, inputs, grid_to_mesh.T, full_in, full_m[0], full_m[1], full_gains, full_dates,
        send_rows[None, :],
    )
    left, right = cyclic(buf, halo)

    out_shape = (variables, LATENT)
    gm_late, gout, gxd, dsum, ggain_late, loss_row, dmesh, dhalo = call(
        main_kernel,
        members,
        [
            scalars,
            scalars,
            node_block,
            node_block,
            per_member((halo, LATENT)),
            per_member((halo, LATENT)),
            per_member((variables, points)),
            per_member((variables, points)),
            whole((members, points)),
            whole((variables, 1)),
            whole(full_dates.shape),
            whole((k_edge, nodes)),
            whole((k_pick, points)),
            whole(full_in.shape),
            whole(full_out.shape),
            matrix,
            matrix,
            matrix,
            matrix,
            matrix,
            whole(full_gains.shape),
        ],
        [
            shape_of((5, LATENT, LATENT), F32),
            shape_of(out_shape, F32),
            shape_of((variables, variables), F32),
            shape_of((members, variables, 1), F32),
            shape_of((2, LATENT), F32),
            shape_of((variables, 1), F32),
            shape_of((members, nodes, LATENT), F32),
            shape_of((members, 2 * halo, LATENT), BF16),
        ],
        [
            whole((5, LATENT, LATENT)),
            whole(out_shape),
            whole((variables, variables)),
            per_member((variables, 1)),
            whole((2, LATENT)),
            whole((variables, 1)),
            node_block,
            per_member((2 * halo, LATENT)),
        ],
        [
            pltpu.VMEM((k_edge * nodes, table), BF16),
            pltpu.VMEM((table, k_edge * nodes), BF16),
            pltpu.VMEM((points, nodes), BF16),
            pltpu.VMEM((nodes, points), BF16),
            pltpu.VMEM((table, LATENT), BF16),
            pltpu.VMEM((k_edge * nodes, LATENT), T_TYPE),
            pltpu.VMEM((2 * nodes, LATENT), BF16),
            pltpu.VMEM((nodes, LATENT), F32),
        ],
        60_000_000_000,
    )(
        (2.0 / valid_count).reshape(1),
        date_index,
        mesh1,
        sent,
        left,
        right,
        inputs,
        targets,
        valid_steps,
        var_weights[:, None],
        full_dates,
        mesh_edges.T,
        mesh_to_grid.T,
        full_in,
        full_out,
        full_m[2],
        full_m[3],
        full_m[4],
        full_m[5],
        full_m[6],
        full_gains,
    )

    from_previous, from_next = cyclic(
        jnp.concatenate([dhalo[:, :halo], dhalo[:, halo:]], axis=1), halo
    )
    returned = jnp.concatenate([from_previous, from_next], axis=1)
    gm_early, gin, ggain_early, gdate = call(
        encode_back_kernel,
        members,
        [
            node_block,
            per_member((2 * halo, LATENT)),
            whole((1, 2 * halo)),
            per_member((nodes, variables)),
            node_block,
            node_block,
            node_block,
            node_block,
            per_member((nodes, 1)),
            matrix,
            matrix,
            whole(full_gains.shape),
            whole(full_out.shape),
            whole((variables, variables)),
            per_member((variables, 1)),
        ],
        [
            shape_of((2, LATENT, LATENT), F32),
            shape_of((variables, LATENT), F32),
            shape_of((1, LATENT), F32),
            shape_of((members, 1, LATENT), F32),
        ],
        [
            whole((2, LATENT, LATENT)),
            whole((variables, LATENT)),
            whole((1, LATENT)),
            per_member((1, LATENT)),
        ],
        [pltpu.VMEM((nodes, 2 * halo), BF16)],
        4_000_000_000,
    )(
        dmesh, returned, send_rows[None, :], x4, a0, h1, t1, unit1, scale1, full_m[0], full_m[1],
        full_gains, full_out, gxd, dsum,
    )

    chosen = (date_index[None, :] == jnp.arange(dates)[:, None]).astype(F32)
    totals = (
        jnp.concatenate([gm_early, gm_late], axis=0),
        gin,
        gout,
        jnp.concatenate([ggain_early, ggain_late], axis=0),
        jnp.dot(chosen, gdate[:, 0, :], precision=HIGHEST),
    )
    reduced = (
        lax.psum_scatter(totals[0], "row", scatter_dimension=1, tiled=True),
        lax.psum_scatter(totals[1], "row", scatter_dimension=1, tiled=True),
        lax.psum_scatter(totals[2], "row", scatter_dimension=1, tiled=True),
        lax.psum_scatter(totals[3], "row", scatter_dimension=1, tiled=True),
        lax.psum_scatter(totals[4], "row", scatter_dimension=1, tiled=True),
    )
    reduced = lax.psum(reduced, "region")
    loss_sum = lax.psum(jnp.sum(loss_row), ("region", "row"))
    g_matrices, g_in, g_out, g_gains, g_dates = reduced
    new_momentum = MUON_MOMENTUM * matrices_momentum + g_matrices
    squares = lax.psum(jnp.sum(new_momentum * new_momentum, axis=(1, 2)), "row")
    current = new_momentum * lax.rsqrt(squares + 1e-07)[:, None, None]
    gram_matrix = gram_sum(current)
    for sweep_index in range(NS_ITERS):
        if sweep_index > 0:
            gram_matrix = gram_sum(current)
        current = sweep_step(current, gram_matrix)
    new_matrices = matrices * (1.0 - MUON_RATE * WEIGHT_DECAY) - MUON_RATE * current
    new_in = adam_update(in_proj, g_in, in_first, in_second, MATRIX_RATE, WEIGHT_DECAY)
    new_out = adam_update(out_proj, g_out.T, out_first, out_second, MATRIX_RATE, WEIGHT_DECAY)
    new_gain = adam_update(norm_gains, g_gains, gains_first, gains_second, VECTOR_RATE, 0.0)
    new_date = adam_update(date_table, g_dates, date_first, date_second, VECTOR_RATE, 0.0)
    return (
        new_matrices,
        new_momentum,
        new_in[0],
        new_in[1],
        new_in[2],
        new_out[0],
        new_out[1],
        new_out[2],
        new_gain[0],
        new_gain[1],
        new_gain[2],
        new_date[0],
        new_date[1],
        new_date[2],
        loss_sum,
        valid_count,
    )


def solution(mesh):
    in_specs = (
        P("row", "region", None),
        P("row", "region", None),
        P("row", "region"),
        P(),
        P("region", None),
        P("region", None),
        P("region"),
        P("region", None),
        P("row"),
        P(None, "row", None),
        P(None, "row", None),
        P(None, "row"),
        P(None, "row"),
        P(None, "row"),
        P("row", None),
        P("row", None),
        P("row", None),
        P(None, "row"),
        P(None, "row"),
        P(None, "row"),
        P(None, "row"),
        P(None, "row"),
        P(None, "row"),
    )
    out_specs = (
        P(None, "row", None),
        P(None, "row", None),
        P(None, "row"),
        P(None, "row"),
        P(None, "row"),
        P("row", None),
        P("row", None),
        P("row", None),
        P(None, "row"),
        P(None, "row"),
        P(None, "row"),
        P(None, "row"),
        P(None, "row"),
        P(None, "row"),
        P(),
        P(),
    )
    return jax.shard_map(body, mesh=mesh, in_specs=in_specs, out_specs=out_specs, check_vma=False)
```

time: 1890 us -> 893 us (0.47)
  other arithmetic: 445 us -> 18.4 us
  local copies, waits for them, and re-layouts: 398 us -> 10.8 us
  matrix products: 387 us -> 40.4 us
  Pallas kernels: 0 us -> 156 us
  blocking collectives: 115 us -> 159 us
  starting transfers between devices: 27.1 us -> 5.11 us
    dot_general x80 -> x3, matrix products: 363 us -> 15.9 us  [the longest x2 15.2 us: gram_sum(): jnp.einsum('mrk,mrl->mkl', block, block, precision=HIGHEST).astype(BF16)]
    scatter-add x12 -> x0, other arithmetic: 263 us -> none  [the longest x3 113 us: decode(): decoded = jnp.mean(mesh_two[mesh_to_grid], axis=1)]
    gather x21 -> x0, local copies, waits for them, and re-layouts: 236 us -> none  [the longest x6 132 us: decode(): decoded = jnp.mean(mesh_two[mesh_to_grid], axis=1)]
    pallas_call x0 -> x3, Pallas kernels: none -> 156 us  [the longest x1 130 us: body(): call(main_kernel, members, [scalars, scalars, node_block, node_block, per...]
    reduce_sum x29 -> x1, other arithmetic: 148 us -> 0.63 us  [body(): loss_sum = lax.psum(jnp.sum(loss_row), ('region', 'row'))]
    broadcast_in_dim x15 -> x1, local copies, waits for them, and re-layouts: 107 us -> 0.79 us  [body(): var_weights[:, None]]
    psum x0 -> x1, blocking collectives: none -> 40 us  [body(): loss_sum = lax.psum(jnp.sum(loss_row), ('region', 'row'))]
    all_gather x1, waiting for transfers between devices: 0.01 us -> 36.1 us  [body(): full_m = lax.all_gather(matrices.astype(BF16), 'row', axis=1, tiled=True)]
  transfers between devices with their start and end apart: 21 -> 13, of which waited for: 7 -> 8; matrix products, arithmetic and copies ran while one was open for 21% -> 4% of each run, Pallas kernels for 0% -> 1%
where the time goes in v1:
time: 893 us; the launch traced here: 887 us
  waiting for transfers between devices  483 us (54%)
  blocking collectives  159 us (18%)
  Pallas kernels  156 us (17%)
  matrix products  40.4 us (5%)
  other arithmetic  18.4 us (2%)
  between operations  15.1 us (2%)
  local copies, waits for them, and re-layouts  10.8 us (1%)
    psum x2, waiting for transfers between devices, gram_sum(): lax.psum(jnp.einsum('mrk,mrl->mkl', block, block, precision=HIGHEST).asty...  233 us
    pallas_call x1, Pallas kernels, body(): call(main_kernel, members, [scalars, scalars, node_block, node_block, per...  130 us
    reduce_scatter x1, waiting for transfers between devices, body(): lax.psum_scatter(totals[0], 'row', scatter_dimension=1, tiled=True)  128 us
    psum x1, waiting for transfers between devices, body(): reduced = lax.psum(reduced, 'region')  65.7 us
    psum x1, blocking collectives, body(): loss_sum = lax.psum(jnp.sum(loss_row), ('region', 'row'))  40 us
    psum x1, blocking collectives, body(): valid_count = lax.psum(jnp.sum(masks), ('region', 'row'))  38.4 us
    all_gather x1, waiting for transfers between devices, body(): full_m = lax.all_gather(matrices.astype(BF16), 'row', axis=1, tiled=True)  36.1 us
  transfers between devices with their start and end apart: 13, of which 8 were waited for; matrix products, arithmetic and copies ran while one was open for 4% of the time, Pallas kernels for 1%

profile of v1, /device:TPU:0, one launch (start us, length us, event | category | flops | bytes accessed | tf_op | source)
XLA Modules:
  0.0 887.4 jit_solution(6065807394948603104)
XLA Ops:
  7.3 2.6 convert_element_type.42
  9.9 12.6 %all_gather.17 = bf16[3,512]{1,0:T(4,128)(2,1)S(1)} all-gather(bf16[3,128]{1,0:T(4,128)(2,1)S(1)} %convert_element_type.43), channel_id=1, replica_groups=mesh['region'=8,'row'=4] {'row'}, dimensions={1}, use_global_device_ids=true | all-gather | bytes 3840 | tf_op jit(solution)/shard_map/all_gather | solution.py:375
  22.6 0.6 convert_element_type.44.gains_ref
  23.2 12.1 %all_gather.18 = bf16[8,512]{1,0:T(8,128)(2,1)S(1)} all-gather(bf16[8,128]{1,0:T(8,128)(2,1)S(1)} %convert_element_type.45), channel_id=1, replica_groups=mesh['region'=8,'row'=4] {'row'}, dimensions={1}, use_global_device_ids=true | all-gather | bytes 10240 | tf_op jit(solution)/shard_map/all_gather | solution.py:376
  35.2 0.6 convert_element_type.46.date_ref
  35.9 16.3 %all_gather.15.win_ref = bf16[227,512]{1,0:T(8,128)(2,1)} all-gather(bf16[227,128]{1,0:T(8,128)(2,1)S(1)} %convert_element_type.41), channel_id=1, replica_groups=mesh['region'=8,'row'=4] {'row'}, dimensions={1}, use_global_device_ids=true | all-gather | bytes 290560 | tf_op jit(solution)/shard_map/all_gather | solution.py:373
  52.1 0.6 convert_reduce_fusion
  52.8 36.1 %all-gather.2.cloned.1.call-done = bf16[7,512,512]{2,1,0:T(8,128)(2,1)} async-done(((bf16[7,128,512]{2,1,0:T(8,128)(2,1)}), bf16[7,512,512]{2,1,0:T(8,128)(2,1)}) %all-gather.2.cloned.1.call-update) | async-done | bytes 3670032 | tf_op jit(solution)/shard_map/all_gather | solution.py:372
  88.9 3.9 slice_bitcast_fusion
  92.8 15.0 %shard_map.342 = (bf16[3,512,227]{2,1,0:T(8,128)(2,1)}, bf16[3,512,512]{2,1,0:T(8,128)(2,1)}, bf16[3,512,512]{2,1,0:T(8,128)(2,1)}, f32[3,512,512]{2,1,0:T(8,128...) custom-call(s32[3]{0:T(128)} %day_ref.3, ...), custom_call_target="tpu_custom_call" | custom-call | flops 6000000000 | bytes 33554432 | tf_op jit(solution)/shard_map/pallas_call | solution.py:381
  107.7 1.1 fusion.41
  108.8 1.9 collective-permute-start.1
  110.7 38.4 %psum.70 = f32[]{:T(128)} all-reduce(f32[]{:T(128)} %convert_reduce_fusion), channel_id=1, replica_groups=mesh['region'=8,'row'=4] {'region','row'}, use_global_device_ids=true, to_apply=%region_1.0 | all-reduce | flops 1 | bytes 8 | tf_op jit(solution)/shard_map/psum | solution.py:371
  149.1 0.8 copy.44.varw_ref
  150.6 13.9 %all_gather.19.wout_ref = bf16[227,512]{1,0:T(8,128)(2,1)} all-gather(bf16[227,128]{1,0:T(8,128)(2,1)S(1)} %convert_bitcast_fusion), channel_id=1, replica_groups=mesh['region'=8,'row'=4] {'row'}, dimensions={1}, use_global_device_ids=true | all-gather | bytes 290560 | tf_op jit(solution)/shard_map/all_gather | solution.py:374
  164.5 0.7 copy-done.25
  165.2 129.5 %shard_map.343 = (f32[5,512,512]{2,1,0:T(8,128)}, f32[227,512]{1,0:T(8,128)}, f32[227,227]{1,0:T(8,128)}, f32[3,227,1]{2,1,0:T(8,128)}, f32[2,512]{1,0:T(2,128)}...) custom-call(f32[1]{0:T(128)} %bitcast.count_ref, s32[3]{0:T(128)} %day_ref.3, ...), custom_call_target="tpu_custom_call" | custom-call | flops 60000002048 | bytes 33554432 | tf_op jit(solution)/shard_map/pallas_call | solution.py:426
  294.8 1.1 fusion.40
  295.9 2.6 collective-permute-start.3
  298.6 3.3 collective-permute-done.2
  301.9 1.1 collective-permute-done.3
  303.0 0.8 pad_maximum_fusion.1.ret_ref
  303.8 11.6 %shard_map.344 = (f32[2,512,512]{2,1,0:T(8,128)}, f32[227,512]{1,0:T(8,128)}, f32[1,512]{1,0:T(1,128)}, f32[3,1,512]{2,1,0:T(1,128)}) custom-call(f32[3,512,512]{2,1,0:T(8,128)} %get-tuple-element.40.dmesh_ref, bf16[3,128,512]{2,1,0:T(8,128)(2,1)} %pad_maximum_fusion.1.ret_ref, s32[1,128]{1,0:T(1,128)} %bitcast.42, ...), custom_call_target="tpu_custom_call" | custom-call | flops 4000000000 | bytes 33554432 | tf_op jit(solution)/shard_map/pallas_call | solution.py:511
  315.5 7.4 pad_maximum_fusion
  322.9 14.8 %reduce-scatter.10.cloned.1.call-done = f32[227,128]{1,0:T(8,128)} async-done(((f32[227,512]{1,0:T(8,128)}), f32[227,128]{1,0:T(8,128)}) %reduce-scatter.10.cloned.1.call-update) | async-done | bytes 116240 | tf_op jit(solution)/shard_map/reduce_scatter | solution.py:560
  337.7 128.3 %reduce-scatter.8.cloned.1.call-done = f32[7,128,512]{2,1,0:T(8,128)} async-done(((f32[7,512,512]{2,1,0:T(8,128)}), f32[7,128,512]{2,1,0:T(8,128)}) %reduce-scatter.8.cloned.1.call-update) | async-done | bytes 1835024 | tf_op jit(solution)/shard_map/reduce_scatter | solution.py:559
  466.1 65.7 %all-reduce.10.cloned.1.call-done = (f32[7,128,512]{2,1,0:T(8,128)}, f32[227,128]{1,0:T(8,128)}, f32[128,227]{0,1:T(8,128)}) async-done(((f32[7,128,512]{2,1,0:T(8,128)}, f32[227,128]{1,0:T(8,128)}, f32[128,227]{0,1:T(8,128)}), (f32[7,128,512]{2,1,0:T(8,128)}, f32[227,128]{1,0:T(8,128)}, f32[128,227]{0,1:T(8,128)})) %all-reduce.10.cloned.1.call-update) | async-done | bytes 2067472 | tf_op jit(solution)/shard_map/psum | solution.py:565
  531.8 2.4 multiply_reduce_fusion
  534.2 11.5 %psum.72 = f32[7]{0:T(128)S(1)} all-reduce(f32[7]{0:T(128)S(1)} %get-tuple-element.75), channel_id=1, replica_groups=mesh['region'=8,'row'=4] {'row'}, use_global_device_ids=true, to_apply=%region_5.0 | all-reduce | flops 7 | bytes 56 | tf_op jit(solution)/shard_map/psum | solution.py:569
  545.7 7.8 convolution_convert_fusion.1
  554.2 0.9 copy.49
  555.2 0.7 fusion.26
  556.2 132.2 %all-reduce.6.cloned.1.call-done = bf16[7,512,512]{2,1,0:T(8,128)(2,1)} async-done(((bf16[7,512,512]{2,1,0:T(8,128)(2,1)}), bf16[7,512,512]{2,1,0:T(8,128)(2,1)}) %all-reduce.6.cloned.1.call-update) | async-done | bytes 3670032 | tf_op jit(solution)/shard_map/psum | solution.py:313
  688.3 5.4 fusion.42
  693.7 7.2 multiply_add_fusion
  701.0 7.4 convolution_convert_fusion
  708.5 0.8 copy-done.12
  709.3 0.6 reduce_sum.29
  709.9 40.0 %psum.79 = f32[]{:T(128)} all-reduce(f32[]{:T(128)} %reduce_sum.29), channel_id=1, replica_groups=mesh['region'=8,'row'=4] {'region','row'}, use_global_device_ids=true, to_apply=%region_17.0 | all-reduce | flops 1 | bytes 8 | tf_op jit(solution)/shard_map/psum | solution.py:566
  750.0 0.9 copy.50
  750.9 14.1 %all-reduce = (f32[3,128]{1,0:T(4,128)S(1)}, f32[8,128]{1,0:T(8,128)S(1)}) all-reduce(f32[3,128]{1,0:T(4,128)S(1)} %copy.50, f32[8,128]{1,0:T(8,128)} %reduce-scatter.14.cloned.1.call-done), channel_id=1, replica_groups=mesh['region'=8,'row'=4] {'region'}, use_global_device_ids=true, to_apply=%region_13.0 | all-reduce | flops 1408 | bytes 11264 | tf_op jit(solution)/shard_map/psum | solution.py:565
  765.0 0.6 divide_subtract_fusion.3
  765.6 0.6 divide_subtract_fusion.2
  766.3 0.8 divide_subtract_fusion.1
  767.0 0.8 divide_subtract_fusion
  767.8 100.9 %all-reduce.8.cloned.1.call-done = bf16[7,512,512]{2,1,0:T(8,128)(2,1)} async-done(((bf16[7,512,512]{2,1,0:T(8,128)(2,1)}), bf16[7,512,512]{2,1,0:T(8,128)(2,1)}) %all-reduce.8.cloned.1.call-update) | async-done | bytes 3670032 | tf_op jit(solution)/shard_map/psum | solution.py:313
  868.7 5.4 fusion.43
  874.1 6.5 multiply_subtract_fusion
  (83 shorter events, 1.6 us)
Async XLA Ops:
  7.2 2.7 copy-start.16
  7.2 2.7 copy-start.14
  7.2 28.7 %copy-start.4 = (f32[227,128]{1,0:T(8,128)S(1)}, f32[227,128]{1,0:T(8,128)}, u32[]{:S(2)}) copy-start(f32[227,128]{1,0:T(8,128)} %param.34) | copy-start | bytes 348676
  7.2 44.9 %copy-start.13 = (s32[3,2048]{1,0:T(4,128)S(1)}, s32[3,2048]{1,0:T(4,128)}, u32[]{:S(2)}) copy-start(s32[3,2048]{1,0:T(4,128)} %valid_ref.1) | copy-start | bytes 73732
  7.2 81.6 %all-gather.2.cloned.1.call-start = ((), (), s32[]{:S(2)}) async-start(), calls=%async_computation.5 | async-start | bytes 4587520 | tf_op jit(solution)/shard_map/all_gather | solution.py:372
  9.8 313.1 %reduce-scatter.12.cloned.1.call-start = ((), (), s32[]{:S(2)}) async-start(), calls=%async_computation.10 | async-start | bytes 593920 | tf_op jit(solution)/shard_map/reduce_scatter | solution.py:561
  92.7 17.9 %copy-start.5 = (f32[128,227]{0,1:T(8,128)S(1)}, f32[128,227]{0,1:T(8,128)}, u32[]{:S(2)}) copy-start(f32[128,227]{0,1:T(8,128)} %param.37) | copy-start | bytes 348676
  92.8 56.3 %copy-start.23 = (f32[227]{0:T(256)S(1)}, f32[227]{0:T(256)}, u32[]{:S(2)}) copy-start(f32[227]{0:T(256)} %param.26) | copy-start | bytes 2728
  108.8 55.7 %collective-permute-start.1 = (bf16[3,64,512]{2,1,0:T(8,128)(2,1)S(1)}, bf16[3,64,512]{2,1,0:T(8,128)(2,1)S(1)}, u32[]{:S(2)}, u32[]{:S(2)}) collective-permute-start(bf16[3,64,512]{2,1,0:T(8,128)(2,1)S(1)} %get-tuple-element.86), channel_id=1, source_target_pairs={{4,0},{8,4},{12,8},{16,12},{20,16},{24,20},{28,24},{0,28},{5,1},{9... | collective-permute-start | bytes 589832 | tf_op jit(solution)/shard_map/ppermute | solution.py:308
  110.7 53.8 %collective-permute-start = (bf16[3,64,512]{2,1,0:T(8,128)(2,1)S(1)}, bf16[3,64,512]{2,1,0:T(8,128)(2,1)S(1)}, u32[]{:S(2)}, u32[]{:S(2)}) collective-permute-start(bf16[3,64,512]{2,1,0:T(8,128)(2,1)S(1)} %get-tuple-element.87), channel_id=1, source_target_pairs={{0,4},{4,8},{8,12},{12,16},{16,20},{20,24},{24,28},{28,0},{1,5},{5... | collective-permute-start | bytes 589832 | tf_op jit(solution)/shard_map/ppermute | solution.py:307
  164.4 0.7 copy-start.25
  164.4 0.7 copy-start.26
  294.8 42.9 %reduce-scatter.10.cloned.1.call-start = ((), (), s32[]{:S(2)}) async-start(), calls=%async_computation.9 | async-start | bytes 593920 | tf_op jit(solution)/shard_map/reduce_scatter | solution.py:560
  295.9 6.0 collective-permute-start.2
  295.9 7.0 collective-permute-start.3
  315.4 150.6 %reduce-scatter.8.cloned.1.call-start = ((), (), s32[]{:S(2)}) async-start(), calls=%async_computation.6 | async-start | bytes 9175040 | tf_op jit(solution)/shard_map/reduce_scatter | solution.py:559
  322.9 208.9 %all-reduce.10.cloned.1.call-start = ((), (), s32[]{:S(2)}) async-start(), calls=%async_computation.13 | async-start | bytes 4145152 | tf_op jit(solution)/shard_map/psum | solution.py:565
  466.0 222.3 %all-reduce.6.cloned.1.call-start = ((), (), s32[]{:S(2)}) async-start(), calls=%async_computation.7 | async-start | bytes 7340032 | tf_op jit(solution)/shard_map/psum | solution.py:313
  534.2 19.3 %copy-start.2 = (f32[7,128,512]{2,1,0:T(8,128)}, f32[7,128,512]{2,1,0:T(8,128)S(1)}, u32[]{:S(2)}) copy-start(f32[7,128,512]{2,1,0:T(8,128)S(1)} %get-tuple-element.76) | copy-start | bytes 5505028
  553.5 0.7 copy-start.19
  553.5 0.7 copy-start.22
  553.5 1.6 copy-start.15
  553.5 1.6 copy-start.24
  553.6 196.4 %reduce-scatter.16.cloned.1.call-start = ((), (), s32[]{:S(2)}) async-start(), calls=%async_computation.12 | async-start | bytes 327680
  555.1 195.7 %reduce-scatter.14.cloned.1.call-start = ((), (), s32[]{:S(2)}) async-start(), calls=%async_computation.11 | async-start | bytes 20480 | tf_op jit(solution)/shard_map/reduce_scatter | solution.py:563
  555.9 312.8 %all-reduce.8.cloned.1.call-start = ((), (), s32[]{:S(2)}) async-start(), calls=%async_computation.8 | async-start | bytes 7340032 | tf_op jit(solution)/shard_map/psum | solution.py:313
  688.3 5.4 copy-start
  708.4 0.9 copy-start.12
  708.4 56.6 %copy-start.20 = (f32[3,128]{1,0:T(4,128)S(1)}, f32[3,128]{1,0:T(4,128)}, u32[]{:S(2)}) copy-start(f32[3,128]{1,0:T(4,128)} %param.41) | copy-start | bytes 4612
  708.4 56.6 %copy-start.21 = (f32[3,128]{1,0:T(4,128)S(1)}, f32[3,128]{1,0:T(4,128)}, u32[]{:S(2)}) copy-start(f32[3,128]{1,0:T(4,128)} %param.42) | copy-start | bytes 4612
  708.4 57.2 %copy-start.17 = (f32[8,128]{1,0:T(8,128)S(1)}, f32[8,128]{1,0:T(8,128)}, u32[]{:S(2)}) copy-start(f32[8,128]{1,0:T(8,128)} %param.44) | copy-start | bytes 12292
  708.4 57.2 %copy-start.18 = (f32[8,128]{1,0:T(8,128)S(1)}, f32[8,128]{1,0:T(8,128)}, u32[]{:S(2)}) copy-start(f32[8,128]{1,0:T(8,128)} %param.45) | copy-start | bytes 12292
  708.4 57.9 %copy-start.6 = (f32[227,128]{1,0:T(8,128)S(1)}, f32[227,128]{1,0:T(8,128)}, u32[]{:S(2)}) copy-start(f32[227,128]{1,0:T(8,128)} %param.35) | copy-start | bytes 348676
  708.4 57.8 %copy-start.7 = (f32[227,128]{1,0:T(8,128)S(1)}, f32[227,128]{1,0:T(8,128)}, u32[]{:S(2)}) copy-start(f32[227,128]{1,0:T(8,128)} %param.36) | copy-start | bytes 348676
  708.4 57.8 %copy-start.11 = (f32[227,128]{1,0:T(8,128)S(1)}, f32[227,128]{1,0:T(8,128)}, u32[]{:S(2)}) copy-start(f32[227,128]{1,0:T(8,128)} %get-tuple-element.61) | copy-start | bytes 348676
  708.4 58.6 %copy-start.8 = (f32[128,227]{0,1:T(8,128)S(1)}, f32[128,227]{0,1:T(8,128)}, u32[]{:S(2)}) copy-start(f32[128,227]{0,1:T(8,128)} %param.38) | copy-start | bytes 348676
  708.4 58.6 %copy-start.9 = (f32[128,227]{0,1:T(8,128)S(1)}, f32[128,227]{0,1:T(8,128)}, u32[]{:S(2)}) copy-start(f32[128,227]{0,1:T(8,128)} %param.39) | copy-start | bytes 348676
  708.5 58.6 %copy-start.10 = (f32[128,227]{0,1:T(8,128)S(1)}, f32[128,227]{0,1:T(8,128)}, u32[]{:S(2)}) copy-start(f32[128,227]{0,1:T(8,128)} %get-tuple-element.62) | copy-start | bytes 348676
  868.7 5.4 copy-start.1
  868.7 5.4 copy-start.3
Sparse Core Ops, SparseCore 0:
  10.2 78.6 all-gather.1
  294.9 20.6 reduce-scatter.11
  318.0 19.7 reduce-scatter.9
  339.9 126.0 reduce-scatter.7
  469.4 62.3 all-reduce.9
  553.7 134.6 all-reduce.5
  691.2 18.6 reduce-scatter.15
  712.8 17.0 reduce-scatter.13
  732.3 136.3 all-reduce.7

commit v2 on v1

--- a/solution.py
+++ b/solution.py
@@ -20,11 +20,13 @@
 
 F32 = jnp.float32
 BF16 = jnp.bfloat16
-HIGHEST = lax.Precision.HIGHEST
 LATENT = 512
 BLOCK = 512
 T_TYPE = F32
 VMEM_BYTES = 60 * 1024 * 1024
+MESH = pl.DeviceIdType.MESH
+SLOTS = 8
+IN_ROW, OUT_ROW, GAIN_ROW, DATE_ROW, LOSS_ROW = 0, 240, 480, 496, 504
 
 
 def dot(left, right):
@@ -71,6 +73,16 @@
     return total.astype(BF16)
 
 
+def gain_row(small_ref, k):
+    return small_ref[GAIN_ROW : GAIN_ROW + 16, :].astype(F32)[k : k + 1, :]
+
+
+def date_row(small_ref, day_ref):
+    table = small_ref[DATE_ROW : DATE_ROW + 16, :].astype(F32)
+    lines = lax.broadcasted_iota(jnp.int32, table.shape, 0)
+    return jnp.sum(jnp.where(lines == day_ref[pl.program_id(0)], table, 0.0), axis=0, keepdims=True)
+
+
 def columns_of(index):
     short = 8 - index.shape[0]
     if short > 0:
@@ -88,7 +100,7 @@
 
 
 def encode_kernel(
-    day_ref, x_ref, picks_ref, win_ref, m0_ref, m1_ref, gains_ref, date_ref, send_ref,
+    day_ref, x_ref, picks_ref, small_ref, m0_ref, m1_ref, send_ref,
     x4_ref, a0_ref, h1_ref, t1_ref, unit_ref, scale_ref, mesh_ref, sent_ref, buf_ref,
     pick_ref, out_ref,
 ):
@@ -100,15 +112,15 @@
 
     x4 = dot_nt(pick_ref[...], x_ref[0]) * (1.0 / picks_ref.shape[0])
     high, low = split_two(x4)
-    win = win_ref[...]
-    agg = dot(high, win) + dot(low, win) + date_ref[pl.ds(day_ref[pl.program_id(0)], 1), :]
+    win = small_ref[IN_ROW : IN_ROW + x_ref.shape[1], :]
+    agg = dot(high, win) + dot(low, win) + date_row(small_ref, day_ref)
     a0 = agg.astype(BF16)
-    pre = dot(a0, m0_ref[...])
+    pre = dot(a0, m0_ref[0])
     gate = sigmoid(pre)
     hid = pre * gate
     h1 = hid.astype(BF16)
-    unit, scale = normalise(dot(h1, m1_ref[...]))
-    mesh = agg + unit * gains_ref[0:1, :]
+    unit, scale = normalise(dot(h1, m1_ref[0]))
+    mesh = agg + unit * gain_row(small_ref, 0)
     sent = mesh.astype(BF16)
     x4_ref[0] = high
     a0_ref[0] = a0
@@ -122,15 +134,14 @@
 
 
 def main_kernel(
-    count_ref, day_ref, mesh_ref, sent_ref, left_ref, right_ref, x_ref, y_ref, valid_ref, varw_ref,
-    date_ref, edge_ref, pick_row_ref,
-    win_ref, wout_ref, m2_ref, m3_ref, m4_ref, m5_ref, m6_ref, gains_ref,
-    gm_ref, gout_ref, gxd_ref, dsum_ref, ggain_ref, loss_ref, dmesh_ref, dhalo_ref,
-    eh_ref, eht_ref, d_ref, dt_ref, ext_ref, t_ref, mm_ref, acc_ref,
+    day_ref, mesh_ref, sent_ref, left_ref, right_ref, x_ref, y_ref, valid_ref, varw_ref,
+    edge_ref, pick_row_ref, small_ref, m2_ref, m3_ref, m4_ref, m5_ref, m6_ref,
+    slots_ref, gout_ref, gxd_ref, dsum_ref, ggain_ref, loss_ref, dmesh_ref, dhalo_ref,
+    gm_ref, out_sem, eh_ref, eht_ref, d_ref, dt_ref, ext_ref, t_ref, mm_ref, acc_ref,
 ):
     nodes = mesh_ref.shape[1]
     table = ext_ref.shape[0]
-    points = x_ref.shape[2]
+    variables, points = x_ref.shape[1:]
     k_edge = edge_ref.shape[0]
     k_pick = pick_row_ref.shape[0]
     halo = left_ref.shape[1]
@@ -161,13 +172,13 @@
     ext_ref[:nodes, :] = sent
     ext_ref[nodes : nodes + halo, :] = left_ref[0]
     ext_ref[nodes + halo :, :] = right_ref[0]
-    receivers = dot(sent, m3_ref[...])
+    receivers = dot(sent, m3_ref[0])
 
     def edge(k, carry):
         hid_sum, t_sum = carry
         rows = pl.ds(pl.multiple_of(k * nodes, nodes), nodes)
         picked = dot(eh_ref[rows, :], ext_ref[...]).astype(BF16)
-        pre = dot(picked, m2_ref[...]) + receivers
+        pre = dot(picked, m2_ref[0]) + receivers
         gate = sigmoid(pre)
         hid = pre * gate
         t = gate + hid * (1.0 - gate)
@@ -177,9 +188,10 @@
     zero = jnp.zeros((nodes, LATENT), F32)
     hid_sum, t_sum = lax.fori_loop(0, k_edge, edge, (zero, zero))
     h_high, h_low = split_two(hid_sum * (1.0 / k_edge))
-    m4 = m4_ref[...]
+    m4 = m4_ref[0]
+    gain2 = gain_row(small_ref, 1)
     unit2, scale2 = normalise(dot(h_high, m4) + dot(h_low, m4))
-    mesh2 = mesh_ref[0] + unit2 * gains_ref[1:2, :]
+    mesh2 = mesh_ref[0] + unit2 * gain2
     m_high, m_low = split_two(mesh2)
     mm_ref[:nodes, :] = m_high
     mm_ref[nodes:, :] = m_low
@@ -187,8 +199,9 @@
     acc_ref[...] = jnp.zeros_like(acc_ref)
     dsum_ref[...] = jnp.zeros_like(dsum_ref)
     member = pl.program_id(0)
-    date = date_ref[pl.ds(day_ref[member], 1), :]
-    gain3 = gains_ref[2:3, :]
+    date = date_row(small_ref, day_ref)
+    gain3 = gain_row(small_ref, 2)
+    wout = small_ref[OUT_ROW : OUT_ROW + variables, :]
     varw = varw_ref[...]
 
     def grid_block(i, carry):
@@ -196,31 +209,30 @@
         picks = d_ref[rows, :]
         dec = dot(picks, mm_ref[:nodes, :]) + dot(picks, mm_ref[nodes:, :])
         a2 = (dec * (1.0 / k_pick)).astype(BF16)
-        pre = dot(a2, m5_ref[...])
+        pre = dot(a2, m5_ref[0])
         gate = sigmoid(pre)
         hid = pre * gate
         t = gate + hid * (1.0 - gate)
         h2 = hid.astype(BF16)
-        unit, scale = normalise(dot(h2, m6_ref[...]))
+        unit, scale = normalise(dot(h2, m6_ref[0]))
         x = x_ref[0, :, rows]
-        grid = dot_tn(x, win_ref[...]) + date + unit * gain3
+        grid = dot_tn(x, small_ref[IN_ROW : IN_ROW + variables, :]) + date + unit * gain3
         grid = grid.astype(BF16)
-        misfit = x.astype(F32) + dot_nt(wout_ref[...], grid) - y_ref[0, :, rows].astype(F32)
+        misfit = x.astype(F32) + dot_nt(wout, grid) - y_ref[0, :, rows].astype(F32)
         valid = valid_ref[pl.ds(member, 1), rows].astype(F32)
         weighted = valid * varw * misfit
         loss_ref[...] += jnp.sum(weighted * misfit, axis=1, keepdims=True)
-        dp = weighted * count_ref[0]
-        dsum_ref[0] += jnp.sum(dp, axis=1, keepdims=True)
-        dp = dp.astype(BF16)
+        dsum_ref[0] += jnp.sum(weighted, axis=1, keepdims=True)
+        dp = weighted.astype(BF16)
         gout_ref[...] += dot(dp, grid)
         gxd_ref[...] += dot_nt(x, dp)
-        dgrid = dot_tn(dp, wout_ref[...])
+        dgrid = dot_tn(dp, wout)
         ggain_ref[1:2, :] += jnp.sum(dgrid * unit, axis=0, keepdims=True)
         dc = norm_back(dgrid, gain3, unit, scale).astype(BF16)
         gm_ref[4] += dot_tn(h2, dc)
-        du = (dot_nt(dc, m6_ref[...]) * t).astype(BF16)
+        du = (dot_nt(dc, m6_ref[0]) * t).astype(BF16)
         gm_ref[3] += dot_tn(a2, du)
-        ddec = dot_nt(du, m5_ref[...]).astype(BF16)
+        ddec = dot_nt(du, m5_ref[0]).astype(BF16)
         acc_ref[...] += dot(dt_ref[:, rows], ddec)
         return carry
 
@@ -228,9 +240,9 @@
 
     dmesh2 = acc_ref[...] * (1.0 / k_pick)
     ggain_ref[0:1, :] += jnp.sum(dmesh2 * unit2, axis=0, keepdims=True)
-    dagg = norm_back(dmesh2, gains_ref[1:2, :], unit2, scale2).astype(BF16)
+    dagg = norm_back(dmesh2, gain2, unit2, scale2).astype(BF16)
     gm_ref[2] += dot_tn(h_high, dagg)
-    dhid = dot_nt(dagg, m4_ref[...]) * (1.0 / k_edge)
+    dhid = dot_nt(dagg, m4_ref[0]) * (1.0 / k_edge)
     dr = (dhid * t_sum).astype(BF16)
     gm_ref[1] += dot_tn(sent, dr)
 
@@ -241,36 +253,60 @@
 
     ds = lax.fori_loop(0, k_edge, edge_back, jnp.zeros((table, LATENT), F32)).astype(BF16)
     gm_ref[0] += dot_tn(ext_ref[...], ds)
-    dext = dot_nt(ds, m2_ref[...])
-    dmesh_ref[0] = dmesh2 + dext[:nodes, :] + dot_nt(dr, m3_ref[...])
+    dext = dot_nt(ds, m2_ref[0])
+    dmesh_ref[0] = dmesh2 + dext[:nodes, :] + dot_nt(dr, m3_ref[0])
     dhalo_ref[0] = dext[nodes:, :].astype(BF16)
 
+    @pl.when(member == pl.num_programs(0) - 1)
+    def _():
+        copy = pltpu.make_async_copy(gm_ref, slots_ref.at[2:7], out_sem)
+        copy.start()
+        copy.wait()
+
 
 def encode_back_kernel(
-    dmesh_ref, ret_ref, send_ref, x4_ref, a0_ref, h1_ref, t1_ref, unit_ref, scale_ref, m0_ref, m1_ref,
-    gains_ref, wout_ref, gxd_ref, dsum_ref, gm_ref, gin_ref, ggain_ref, gdate_ref, back_ref,
+    day_ref, slots_in_ref, dmesh_ref, ret_ref, send_ref, x4_ref, a0_ref, h1_ref, t1_ref, unit_ref,
+    scale_ref, m0_ref, m1_ref, small_ref, gxd_ref, dsum_ref, gout_ref, ggain_ref, loss_ref,
+    slots_ref, gm_ref, pack_ref, back_ref, out_sem,
 ):
-    @pl.when(pl.program_id(0) == 0)
+    variables = gxd_ref.shape[0]
+    wout = small_ref[OUT_ROW : OUT_ROW + variables, :]
+    member = pl.program_id(0)
+
+    @pl.when(member == 0)
     def _():
         back_ref[...] = count_rows(send_ref[...], back_ref.shape[0])
         gm_ref[...] = jnp.zeros_like(gm_ref)
-        ggain_ref[...] = jnp.zeros_like(ggain_ref)
+        pack_ref[...] = jnp.zeros_like(pack_ref)
         high, low = split_two(gxd_ref[...])
-        wout = wout_ref[...]
-        gin_ref[...] = dot(high, wout) + dot(low, wout)
+        pack_ref[IN_ROW : IN_ROW + variables, :] = dot(high, wout) + dot(low, wout)
+        pack_ref[OUT_ROW : OUT_ROW + variables, :] = gout_ref[...]
+        pack_ref[GAIN_ROW + 1 : GAIN_ROW + 3, :] = ggain_ref[...]
+        loss = jnp.sum(loss_ref[...], axis=0, keepdims=True)
+        pack_ref[LOSS_ROW : LOSS_ROW + 1, :] = jnp.broadcast_to(loss, (1, pack_ref.shape[1]))
 
     dmesh = dmesh_ref[0] + dot(back_ref[...], ret_ref[0])
     unit = unit_ref[0]
-    ggain_ref[...] += jnp.sum(dmesh * unit, axis=0, keepdims=True)
-    dc = norm_back(dmesh, gains_ref[0:1, :], unit, scale_ref[0]).astype(BF16)
+    pack_ref[GAIN_ROW : GAIN_ROW + 1, :] += jnp.sum(dmesh * unit, axis=0, keepdims=True)
+    dc = norm_back(dmesh, gain_row(small_ref, 0), unit, scale_ref[0]).astype(BF16)
     gm_ref[1] += dot_tn(h1_ref[0], dc)
-    du = (dot_nt(dc, m1_ref[...]) * t1_ref[0]).astype(BF16)
+    du = (dot_nt(dc, m1_ref[0]) * t1_ref[0]).astype(BF16)
     gm_ref[0] += dot_tn(a0_ref[0], du)
-    dagg = dmesh + dot_nt(du, m0_ref[...])
-    gin_ref[...] += dot_tn(x4_ref[0], dagg.astype(BF16))
+    dagg = dmesh + dot_nt(du, m0_ref[0])
+    pack_ref[IN_ROW : IN_ROW + variables, :] += dot_tn(x4_ref[0], dagg.astype(BF16))
     high, low = split_two(dsum_ref[0])
-    wout = wout_ref[...]
-    gdate_ref[0] = jnp.sum(dagg, axis=0, keepdims=True) + dot_tn(high, wout) + dot_tn(low, wout)
+    date = jnp.sum(dagg, axis=0, keepdims=True) + dot_tn(high, wout) + dot_tn(low, wout)
+    pack_ref[pl.ds(DATE_ROW + day_ref[member], 1), :] += date
+
+    @pl.when(member == pl.num_programs(0) - 1)
+    def _():
+        pack_ref[...] = jnp.transpose(pack_ref[...])
+        first = pltpu.make_async_copy(gm_ref, slots_ref.at[0:2], out_sem.at[0])
+        second = pltpu.make_async_copy(pack_ref, slots_ref.at[7], out_sem.at[1])
+        first.start()
+        second.start()
+        first.wait()
+        second.wait()
 
 
 def whole(shape):
@@ -281,7 +317,7 @@
     return pl.BlockSpec((1,) + shape, lambda m: (m, 0, 0))
 
 
-def call(kernel, members, in_specs, out_shapes, out_specs, scratch, cost):
+def call(kernel, members, in_specs, out_shapes, out_specs, scratch, cost, aliases=None):
     return pl.pallas_call(
         kernel,
         grid=(members,),
@@ -289,6 +325,7 @@
         out_shape=out_shapes,
         out_specs=out_specs,
         scratch_shapes=scratch,
+        input_output_aliases=aliases or {},
         compiler_params=pltpu.CompilerParams(
             dimension_semantics=("arbitrary",), vmem_limit_bytes=VMEM_BYTES
         ),
@@ -298,6 +335,357 @@
 
 def shape_of(shape, dtype):
     return jax.ShapeDtypeStruct(shape, dtype)
+
+
+def neighbours():
+    region = lax.axis_index("region")
+    slot = lax.rem(region, SLOTS)
+    base = region - slot
+    one = lax.rem(slot, 2)
+    two = lax.rem(slot // 2, 2)
+    four = slot // 4
+    core = slot + 1 - 2 * one
+    side = slot + 2 - 4 * two
+    up = slot + 4 - 8 * four
+    far = side + 4 - 8 * four
+    return base, slot, core, side, up, far
+
+
+def remote(source, target, send, receive, where):
+    return pltpu.make_async_remote_copy(
+        src_ref=source, dst_ref=target, send_sem=send, recv_sem=receive,
+        device_id=where, device_id_type=MESH,
+    )
+
+
+def greet(places):
+    barrier = pltpu.get_barrier_semaphore()
+    for place in places:
+        pl.semaphore_signal(barrier, inc=1, device_id=place, device_id_type=MESH)
+    pl.semaphore_wait(barrier, len(places))
+
+
+def gather_kernel(
+    depth, block_ref, count_ref, full_ref, total_ref, counts_ref, sums_ref, heard_ref,
+    local_sem, z_send, z_recv, p_send, p_recv, d_send, d_recv, c_send, c_recv, n_send, n_recv,
+    s_send, s_recv,
+):
+    base, slot, core, side, up, far = neighbours()
+    z = lax.axis_index("row")
+    half = block_ref.shape[1] // 2
+    low, high = pl.ds(0, half), pl.ds(half, half)
+    to_core, to_side, to_up = ({"region": base + place} for place in (core, side, up))
+    to_z = [None] + [{"row": lax.rem(z + d, depth)} for d in range(1, depth)]
+    source = [z] + [lax.rem(z + depth - d, depth) for d in range(1, depth)]
+    steps = range(1, depth)
+    greet(to_z[1:] + [to_core, to_side, to_up])
+
+    own = pltpu.make_async_copy(block_ref, full_ref.at[:, z], local_sem)
+    sent = []
+
+    def send(*args):
+        copy = remote(*args)
+        copy.start()
+        sent.append(copy)
+
+    def arrived(target, receive):
+        remote(target, target, receive, receive, to_core).wait_recv()
+
+    for d in steps:
+        send(block_ref.at[slot], full_ref.at[slot, z], z_send.at[d], z_recv.at[d], to_z[d])
+    own.start()
+    for d in steps:
+        send(count_ref, counts_ref.at[d], n_send.at[d], n_recv.at[d], to_z[d])
+    for d in steps:
+        chunk = full_ref.at[slot, source[d]]
+        arrived(chunk, z_recv.at[d])
+        send(chunk, chunk, p_send.at[0, d], p_recv.at[0, d], to_side)
+        send(chunk, chunk, p_send.at[1, d], p_recv.at[1, d], to_up)
+        send(chunk, chunk, c_send.at[0, d], c_recv.at[0, d], to_core)
+
+    total = count_ref[...]
+    for d in steps:
+        arrived(counts_ref.at[d], n_recv.at[d])
+        total = total + counts_ref[d]
+    sums_ref[0] = total
+    send(sums_ref.at[0], heard_ref.at[0], s_send.at[0], s_recv.at[0], to_core)
+
+    for d in steps:
+        chunk = full_ref.at[side, source[d]]
+        arrived(chunk, p_recv.at[0, d])
+        part = full_ref.at[side, source[d], low]
+        send(part, part, d_send.at[0, d], d_recv.at[0, d], to_up)
+        send(chunk, chunk, c_send.at[1, d], c_recv.at[1, d], to_core)
+        chunk = full_ref.at[up, source[d]]
+        arrived(chunk, p_recv.at[1, d])
+        part = full_ref.at[up, source[d], high]
+        send(part, part, d_send.at[1, d], d_recv.at[1, d], to_side)
+        send(chunk, chunk, c_send.at[2, d], c_recv.at[2, d], to_core)
+
+    for step, place in ((1, to_side), (2, to_up)):
+        arrived(heard_ref.at[step - 1], s_recv.at[step - 1])
+        total = total + heard_ref[step - 1]
+        sums_ref[step] = total
+        send(sums_ref.at[step], heard_ref.at[step], s_send.at[step], s_recv.at[step], place)
+
+    for d in steps:
+        arrived(full_ref.at[far, source[d], low], d_recv.at[0, d])
+        arrived(full_ref.at[far, source[d], high], d_recv.at[1, d])
+        chunk = full_ref.at[far, source[d]]
+        send(chunk, chunk, c_send.at[3, d], c_recv.at[3, d], to_core)
+    arrived(heard_ref.at[2], s_recv.at[2])
+    total_ref[...] = total + heard_ref[2]
+    for d in steps:
+        for k in range(4):
+            arrived(full_ref.at[core, source[d]], c_recv.at[k, d])
+    for copy in sent:
+        copy.wait_send()
+    own.wait()
+
+
+def gather_weights(block, count, depth):
+    hbm = pl.BlockSpec(memory_space=pl.ANY)
+    vmem = pl.BlockSpec(memory_space=pltpu.VMEM)
+    dma = pltpu.SemaphoreType.DMA
+    rows, width = block.shape[1:]
+    return pl.pallas_call(
+        partial(gather_kernel, depth),
+        in_specs=[vmem, vmem],
+        out_shape=[
+            shape_of((SLOTS, depth, rows, width), BF16),
+            shape_of(count.shape, F32),
+        ],
+        out_specs=[hbm, vmem],
+        scratch_shapes=[
+            pltpu.VMEM((depth,) + count.shape, F32),
+            pltpu.VMEM((3,) + count.shape, F32),
+            pltpu.VMEM((3,) + count.shape, F32),
+            dma,
+            dma((depth,)),
+            dma((depth,)),
+            dma((2, depth)),
+            dma((2, depth)),
+            dma((2, depth)),
+            dma((2, depth)),
+            dma((4, depth)),
+            dma((4, depth)),
+            dma((depth,)),
+            dma((depth,)),
+            dma((3,)),
+            dma((3,)),
+        ],
+        compiler_params=pltpu.CompilerParams(
+            collective_id=0, has_side_effects=True, vmem_limit_bytes=VMEM_BYTES
+        ),
+    )(block, count)
+
+
+def reduce_kernel(
+    depth, slots_ref, momentum_ref, count_ref, g_ref, x_ref,
+    own_ref, heard_ref, snd_ref, rcv_ref, snd_low_ref, rcv_low_ref, acc_ref, zr_ref, g_own_ref,
+    mb_ref, x_own_ref,
+    l_sem, h_send, h_recv, p_send, p_recv, q_send, q_recv, z_send, z_recv, m_send, m_recv,
+    g_local, g_send, g_recv, x_local, x_send, x_recv,
+):
+    base, slot, core, side, up, far = neighbours()
+    z = lax.axis_index("row")
+    rows = acc_ref.shape[0] // depth
+    places = (far, side, up, slot)
+    to_core, to_side, to_up, to_far = ({"region": base + place} for place in (core, side, up, far))
+    to_place = (to_far, to_side, to_up)
+    to_z = [None] + [{"row": lax.rem(z + d, depth)} for d in range(1, depth)]
+    greet(to_z[1:] + [to_core, to_side, to_up, to_far])
+    shift = core - slot
+    last = SLOTS - 1
+    sent = []
+
+    def send(*args):
+        copy = remote(*args)
+        copy.start()
+        sent.append(copy)
+
+    def arrived(target, receive):
+        remote(target, target, receive, receive, to_core).wait_recv()
+
+    loads = []
+    for b in range(depth):
+        part = pl.ds(b * rows, rows)
+        for k, place in enumerate(places):
+            send(
+                slots_ref.at[place + shift, part], heard_ref.at[k, part],
+                h_send.at[k, b], h_recv.at[k, b], to_core,
+            )
+            copy = pltpu.make_async_copy(
+                slots_ref.at[place, part], own_ref.at[k, part], l_sem.at[k, b]
+            )
+            copy.start()
+            loads.append(copy)
+
+    for b in range(depth):
+        part = pl.ds(b * rows, rows)
+        for k in range(4):
+            loads[b * 4 + k].wait()
+            arrived(heard_ref.at[k, part], h_recv.at[k, b])
+            total = own_ref[k, part, :] + heard_ref[k, part, :]
+            if k == 3:
+                acc_ref[part, :] = total
+                continue
+            snd_ref[k, part, :] = total.astype(BF16)
+            send(
+                snd_ref.at[k, part], rcv_ref.at[k, part], p_send.at[k, b], p_recv.at[k, b],
+                to_place[k],
+            )
+
+            @pl.when(places[k] == last)
+            def _():
+                snd_low_ref[part, :] = (total - total.astype(BF16).astype(F32)).astype(BF16)
+                remote(
+                    snd_low_ref.at[part], rcv_low_ref.at[k, part], q_send.at[b], q_recv.at[k, b],
+                    to_place[k],
+                ).start()
+
+    for b in range(depth):
+        part = pl.ds(b * rows, rows)
+        total = acc_ref[part, :]
+        for k in range(3):
+            arrived(rcv_ref.at[k, part], p_recv.at[k, b])
+            total = total + rcv_ref[k, part, :].astype(F32)
+        acc_ref[part, :] = total
+
+        @pl.when(slot == last)
+        def _():
+            low = acc_ref[part, :]
+            for k in range(3):
+                arrived(rcv_low_ref.at[k, part], q_recv.at[k, b])
+                low = low + rcv_low_ref[k, part, :].astype(F32)
+            acc_ref[part, :] = low
+
+        @pl.when(z != b)
+        def _():
+            d = lax.rem(b - z + depth, depth)
+            remote(
+                acc_ref.at[part], zr_ref.at[d], z_send.at[b], z_recv.at[d], {"row": b + 0 * z}
+            ).start()
+
+    g_own = acc_ref[pl.ds(pl.multiple_of(z * rows, rows), rows), :]
+    for d in range(1, depth):
+        arrived(zr_ref.at[d], z_recv.at[d])
+        g_own = g_own + zr_ref[d]
+    g_own_ref[...] = g_own
+    momentum = MUON_MOMENTUM * momentum_ref[slot - slot // last] + (2.0 / count_ref[0:1, 0:1]) * g_own
+    mb_ref[0] = momentum.astype(BF16)
+    for d in range(1, depth):
+        send(mb_ref.at[0], mb_ref.at[d], m_send.at[d], m_recv.at[d], to_z[d])
+    g_copy = pltpu.make_async_copy(g_own_ref, g_ref.at[slot], g_local)
+    g_copy.start()
+    for k in range(3):
+        send(g_own_ref, g_ref.at[slot], g_send.at[k], g_recv.at[k], to_place[k])
+    send(g_own_ref, g_ref.at[slot], g_send.at[3], g_recv.at[3], to_core)
+
+    for d in range(1, depth):
+        arrived(mb_ref.at[d], m_recv.at[d])
+    everything = jnp.concatenate([mb_ref[d] for d in range(depth)], axis=0)
+    wide = everything.astype(F32)
+    squares = jnp.sum(jnp.sum(wide * wide, axis=1, keepdims=True), axis=0, keepdims=True)
+    inverse = lax.rsqrt(squares + 1e-07)
+    mine = momentum * inverse
+    current = (wide * inverse).astype(BF16)
+    mine_low = mine.astype(BF16)
+    for sweep in range(NS_ITERS):
+        gram = dot_tn(current, current)
+        gram_low = gram.astype(BF16)
+        mixing = NS_COEFFS[1] * gram + NS_COEFFS[2] * dot(gram_low, gram_low)
+        mixing = mixing.astype(BF16)
+        mine = NS_COEFFS[0] * mine + dot(mine_low, mixing)
+        mine_low = mine.astype(BF16)
+        if sweep < NS_ITERS - 1:
+            current = (NS_COEFFS[0] * current.astype(F32) + dot(current, mixing)).astype(BF16)
+    x_own_ref[...] = mine_low
+    x_copy = pltpu.make_async_copy(x_own_ref, x_ref.at[slot], x_local)
+    x_copy.start()
+    for k in range(3):
+        send(x_own_ref, x_ref.at[slot], x_send.at[k], x_recv.at[k], to_place[k])
+    send(x_own_ref, x_ref.at[slot], x_send.at[3], x_recv.at[3], to_core)
+
+    for target, send_sem, recv_sem in ((g_ref, g_send, g_recv), (x_ref, x_send, x_recv)):
+        for k in range(3):
+            chunk = target.at[places[k]]
+            arrived(chunk, recv_sem.at[k])
+            send(chunk, chunk, send_sem.at[4 + k], recv_sem.at[4 + k], to_core)
+    for target, recv_sem in ((g_ref, g_recv), (x_ref, x_recv)):
+        for k in range(3, 7):
+            arrived(target.at[core], recv_sem.at[k])
+    for copy in sent:
+        copy.wait_send()
+    for b in range(depth):
+        part = pl.ds(b * rows, rows)
+        for k in range(3):
+
+            @pl.when(places[k] == last)
+            def _():
+                remote(
+                    snd_low_ref.at[part], rcv_low_ref.at[k, part], q_send.at[b], q_recv.at[k, b],
+                    to_place[k],
+                ).wait_send()
+
+        @pl.when(z != b)
+        def _():
+            remote(
+                acc_ref.at[part], acc_ref.at[part], z_send.at[b], z_send.at[b], to_core
+            ).wait_send()
+
+    g_copy.wait()
+    x_copy.wait()
+
+
+def reduce_gradients(slots, momentum, count, depth):
+    hbm = pl.BlockSpec(memory_space=pl.ANY)
+    vmem = pl.BlockSpec(memory_space=pltpu.VMEM)
+    dma = pltpu.SemaphoreType.DMA
+    height, width = slots.shape[1:]
+    rows = height // depth
+    return pl.pallas_call(
+        partial(reduce_kernel, depth),
+        in_specs=[hbm, vmem, vmem],
+        out_shape=[
+            shape_of((SLOTS, rows, width), F32),
+            shape_of((SLOTS, rows, width), BF16),
+        ],
+        out_specs=[hbm, hbm],
+        scratch_shapes=[
+            pltpu.VMEM((4, height, width), F32),
+            pltpu.VMEM((4, height, width), F32),
+            pltpu.VMEM((3, height, width), BF16),
+            pltpu.VMEM((3, height, width), BF16),
+            pltpu.VMEM((height, width), BF16),
+            pltpu.VMEM((3, height, width), BF16),
+            pltpu.VMEM((height, width), F32),
+            pltpu.VMEM((depth, rows, width), F32),
+            pltpu.VMEM((rows, width), F32),
+            pltpu.VMEM((depth, rows, width), BF16),
+            pltpu.VMEM((rows, width), BF16),
+            dma((4, depth)),
+            dma((4, depth)),
+            dma((4, depth)),
+            dma((3, depth)),
+            dma((3, depth)),
+            dma((depth,)),
+            dma((3, depth)),
+            dma((depth,)),
+            dma((depth,)),
+            dma((depth,)),
+            dma((depth,)),
+            dma,
+            dma((7,)),
+            dma((7,)),
+            dma,
+            dma((7,)),
+            dma((7,)),
+        ],
+        compiler_params=pltpu.CompilerParams(
+            collective_id=1, has_side_effects=True, vmem_limit_bytes=VMEM_BYTES
+        ),
+    )(slots, momentum, count)
 
 
 def cyclic(block, halo):
@@ -307,18 +695,6 @@
     low = lax.ppermute(block[:, -halo:], "region", forward)
     high = lax.ppermute(block[:, :halo], "region", backward)
     return low, high
-
-
-def gram_sum(block):
-    return lax.psum(
-        jnp.einsum("mrk,mrl->mkl", block, block, precision=HIGHEST).astype(BF16), "row"
-    ).astype(F32)
-
-
-def sweep_step(current, gram_matrix):
-    square = jnp.einsum("mkj,mjl->mkl", gram_matrix, gram_matrix, precision=HIGHEST)
-    mixing = NS_COEFFS[1] * gram_matrix + NS_COEFFS[2] * square
-    return NS_COEFFS[0] * current + jnp.einsum("mrk,mkl->mrl", current, mixing, precision=HIGHEST)
 
 
 def adam_update(weight, gradient, first_moment, second_moment, step_rate, decay_rate):
@@ -367,17 +743,41 @@
     k_pick = mesh_to_grid.shape[1]
     dates = date_table.shape[0]
 
-    masks = valid_steps.astype(F32)
-    valid_count = lax.psum(jnp.sum(masks), ("region", "row"))
-    full_m = lax.all_gather(matrices.astype(BF16), "row", axis=1, tiled=True)
-    full_in = lax.all_gather(in_proj.astype(BF16), "row", axis=1, tiled=True)
-    full_out = lax.all_gather(out_proj.T.astype(BF16), "row", axis=1, tiled=True)
-    full_gains = lax.all_gather(norm_gains.astype(BF16), "row", axis=1, tiled=True).astype(F32)
-    full_dates = lax.all_gather(date_table.astype(BF16), "row", axis=1, tiled=True).astype(F32)
+    depth = lax.axis_size("row")
+    regions = lax.axis_size("region")
+    groups = [[g * SLOTS + q for g in range(regions // SLOTS)] for q in range(SLOTS)]
     scalars = pl.BlockSpec(memory_space=pltpu.SMEM)
+    hbm = pl.BlockSpec(memory_space=pl.ANY)
+    share = matrices.shape[1]
+
+    def stacked(in_part, out_part, gain_part, date_part):
+        blank = lambda rows: jnp.zeros((rows, share), in_part.dtype)
+        return jnp.concatenate(
+            [
+                in_part, blank(OUT_ROW - variables),
+                out_part, blank(GAIN_ROW - OUT_ROW - variables),
+                gain_part, blank(DATE_ROW - GAIN_ROW - gain_part.shape[0]),
+                date_part, blank(LATENT - DATE_ROW - dates),
+            ],
+            axis=0,
+        )
+
+    small = stacked(in_proj, out_proj.T, norm_gains, date_table)
+    block = jnp.concatenate([matrices, small.T[None]], axis=0).astype(BF16)
+    local_count = jnp.full((8, 128), jnp.sum(valid_steps).astype(F32))
+    gathered, count = gather_weights(block, local_count, depth)
+    if regions > SLOTS:
+        count = lax.psum(count, "region", axis_index_groups=groups)
+    valid_count = count[0, 0]
+    weights = gathered.reshape(SLOTS, LATENT, LATENT)
+    small = weights[SLOTS - 1].T
 
     node_block = per_member((nodes, LATENT))
-    matrix = whole((LATENT, LATENT))
+    full_slot = whole((LATENT, LATENT))
+
+    def matrix(j):
+        return pl.BlockSpec((1, LATENT, LATENT), lambda m: (j, 0, 0))
+
     x4, a0, h1, t1, unit1, scale1, mesh1, sent, buf = call(
         encode_kernel,
         members,
@@ -385,11 +785,9 @@
             scalars,
             per_member((variables, points)),
             whole((grid_to_mesh.shape[1], nodes)),
-            whole(full_in.shape),
-            matrix,
-            matrix,
-            whole(full_gains.shape),
-            whole(full_dates.shape),
+            full_slot,
+            matrix(0),
+            matrix(1),
             whole((1, 2 * halo)),
         ],
         [
@@ -417,17 +815,15 @@
         [pltpu.VMEM((nodes, points), BF16), pltpu.VMEM((2 * halo, nodes), BF16)],
         6_000_000_000,
     )(
-        date_index, inputs, grid_to_mesh.T, full_in, full_m[0], full_m[1], full_gains, full_dates,
-        send_rows[None, :],
+        date_index, inputs, grid_to_mesh.T, small, weights, weights, send_rows[None, :],
     )
     left, right = cyclic(buf, halo)
 
     out_shape = (variables, LATENT)
-    gm_late, gout, gxd, dsum, ggain_late, loss_row, dmesh, dhalo = call(
+    slots, gout, gxd, dsum, ggain_late, loss_row, dmesh, dhalo = call(
         main_kernel,
         members,
         [
-            scalars,
             scalars,
             node_block,
             node_block,
@@ -437,20 +833,17 @@
             per_member((variables, points)),
             whole((members, points)),
             whole((variables, 1)),
-            whole(full_dates.shape),
             whole((k_edge, nodes)),
             whole((k_pick, points)),
-            whole(full_in.shape),
-            whole(full_out.shape),
-            matrix,
-            matrix,
-            matrix,
-            matrix,
-            matrix,
-            whole(full_gains.shape),
+            full_slot,
+            matrix(2),
+            matrix(3),
+            matrix(4),
+            matrix(5),
+            matrix(6),
         ],
         [
-            shape_of((5, LATENT, LATENT), F32),
+            shape_of((SLOTS, LATENT, LATENT), F32),
             shape_of(out_shape, F32),
             shape_of((variables, variables), F32),
             shape_of((members, variables, 1), F32),
@@ -460,7 +853,7 @@
             shape_of((members, 2 * halo, LATENT), BF16),
         ],
         [
-            whole((5, LATENT, LATENT)),
+            hbm,
             whole(out_shape),
             whole((variables, variables)),
             per_member((variables, 1)),
@@ -470,6 +863,8 @@
             per_member((2 * halo, LATENT)),
         ],
         [
+            pltpu.VMEM((5, LATENT, LATENT), F32),
+            pltpu.SemaphoreType.DMA,
             pltpu.VMEM((k_edge * nodes, table), BF16),
             pltpu.VMEM((table, k_edge * nodes), BF16),
             pltpu.VMEM((points, nodes), BF16),
@@ -481,7 +876,6 @@
         ],
         60_000_000_000,
     )(
-        (2.0 / valid_count).reshape(1),
         date_index,
         mesh1,
         sent,
@@ -491,27 +885,26 @@
         targets,
         valid_steps,
         var_weights[:, None],
-        full_dates,
         mesh_edges.T,
         mesh_to_grid.T,
-        full_in,
-        full_out,
-        full_m[2],
-        full_m[3],
-        full_m[4],
-        full_m[5],
-        full_m[6],
-        full_gains,
+        small,
+        weights,
+        weights,
+        weights,
+        weights,
+        weights,
     )
 
     from_previous, from_next = cyclic(
         jnp.concatenate([dhalo[:, :halo], dhalo[:, halo:]], axis=1), halo
     )
     returned = jnp.concatenate([from_previous, from_next], axis=1)
-    gm_early, gin, ggain_early, gdate = call(
+    (slots,) = call(
         encode_back_kernel,
         members,
         [
+            scalars,
+            hbm,
             node_block,
             per_member((2 * halo, LATENT)),
             whole((1, 2 * halo)),
@@ -521,58 +914,42 @@
             node_block,
             node_block,
             per_member((nodes, 1)),
-            matrix,
-            matrix,
-            whole(full_gains.shape),
-            whole(full_out.shape),
+            matrix(0),
+            matrix(1),
+            full_slot,
             whole((variables, variables)),
             per_member((variables, 1)),
-        ],
+            whole(out_shape),
+            whole((2, LATENT)),
+            whole((variables, 1)),
+        ],
+        [shape_of(slots.shape, F32)],
+        [hbm],
         [
-            shape_of((2, LATENT, LATENT), F32),
-            shape_of((variables, LATENT), F32),
-            shape_of((1, LATENT), F32),
-            shape_of((members, 1, LATENT), F32),
-        ],
-        [
-            whole((2, LATENT, LATENT)),
-            whole((variables, LATENT)),
-            whole((1, LATENT)),
-            per_member((1, LATENT)),
-        ],
-        [pltpu.VMEM((nodes, 2 * halo), BF16)],
+            pltpu.VMEM((2, LATENT, LATENT), F32),
+            pltpu.VMEM((LATENT, LATENT), F32),
+            pltpu.VMEM((nodes, 2 * halo), BF16),
+            pltpu.SemaphoreType.DMA((2,)),
+        ],
         4_000_000_000,
+        {1: 0},
     )(
-        dmesh, returned, send_rows[None, :], x4, a0, h1, t1, unit1, scale1, full_m[0], full_m[1],
-        full_gains, full_out, gxd, dsum,
+        date_index, slots, dmesh, returned, send_rows[None, :], x4, a0, h1, t1, unit1, scale1, weights,
+        weights, small, gxd, dsum, gout, ggain_late, loss_row,
     )
-
-    chosen = (date_index[None, :] == jnp.arange(dates)[:, None]).astype(F32)
-    totals = (
-        jnp.concatenate([gm_early, gm_late], axis=0),
-        gin,
-        gout,
-        jnp.concatenate([ggain_early, ggain_late], axis=0),
-        jnp.dot(chosen, gdate[:, 0, :], precision=HIGHEST),
-    )
-    reduced = (
-        lax.psum_scatter(totals[0], "row", scatter_dimension=1, tiled=True),
-        lax.psum_scatter(totals[1], "row", scatter_dimension=1, tiled=True),
-        lax.psum_scatter(totals[2], "row", scatter_dimension=1, tiled=True),
-        lax.psum_scatter(totals[3], "row", scatter_dimension=1, tiled=True),
-        lax.psum_scatter(totals[4], "row", scatter_dimension=1, tiled=True),
-    )
-    reduced = lax.psum(reduced, "region")
-    loss_sum = lax.psum(jnp.sum(loss_row), ("region", "row"))
-    g_matrices, g_in, g_out, g_gains, g_dates = reduced
+    if regions > SLOTS:
+        slots = lax.psum(slots, "region", axis_index_groups=groups)
+    sums, turned = reduce_gradients(slots, matrices_momentum, count, depth)
+    rest = sums[SLOTS - 1].T
+    loss_sum = rest[LOSS_ROW, 0]
+    rest = rest * (2.0 / valid_count)
+    g_matrices = sums[: SLOTS - 1] * (2.0 / valid_count)
+    g_in = rest[IN_ROW : IN_ROW + variables]
+    g_out = rest[OUT_ROW : OUT_ROW + variables]
+    g_gains = rest[GAIN_ROW : GAIN_ROW + norm_gains.shape[0]]
+    g_dates = rest[DATE_ROW : DATE_ROW + dates]
+    current = turned[: SLOTS - 1].astype(F32)
     new_momentum = MUON_MOMENTUM * matrices_momentum + g_matrices
-    squares = lax.psum(jnp.sum(new_momentum * new_momentum, axis=(1, 2)), "row")
-    current = new_momentum * lax.rsqrt(squares + 1e-07)[:, None, None]
-    gram_matrix = gram_sum(current)
-    for sweep_index in range(NS_ITERS):
-        if sweep_index > 0:
-            gram_matrix = gram_sum(current)
-        current = sweep_step(current, gram_matrix)
     new_matrices = matrices * (1.0 - MUON_RATE * WEIGHT_DECAY) - MUON_RATE * current
     new_in = adam_update(in_proj, g_in, in_first, in_second, MATRIX_RATE, WEIGHT_DECAY)
     new_out = adam_update(out_proj, g_out.T, out_first, out_second, MATRIX_RATE, WEIGHT_DECAY)

time: 893 us -> 327 us (0.37)
  waiting for transfers between devices: 483 us -> 3.9 us
  blocking collectives: 159 us -> 0 us
  Pallas kernels: 156 us -> 270 us
  matrix products: 40.4 us -> 0 us
  local copies, waits for them, and re-layouts: 10.8 us -> 30.3 us
  between operations: 15.1 us -> 2.36 us
    psum x3 -> x0, waiting for transfers between devices: 299 us -> none  [the longest x2 233 us: gram_sum(): lax.psum(jnp.einsum('mrk,mrl->mkl', block, block, precision=HIGHEST).asty...]
    reduce_scatter x4 -> x0, waiting for transfers between devices: 143 us -> none  [the longest x1 128 us: body(): lax.psum_scatter(totals[0], 'row', scatter_dimension=1, tiled=True)]
    pallas_call x2 -> x4, Pallas kernels: 141 us -> 255 us  [the longest x1 130 us: body(): call(main_kernel, members, [scalars, node_block, node_block, per_member((...]
    psum x4 -> x0, blocking collectives: 104 us -> none  [the longest x1 40 us: body(): loss_sum = lax.psum(jnp.sum(loss_row), ('region', 'row'))]
    all_gather x4 -> x0, blocking collectives: 54.8 us -> none  [the longest x1 16.3 us: body(): full_in = lax.all_gather(in_proj.astype(BF16), 'row', axis=1, tiled=True)]
    dot_general x7 -> x0, matrix products: 40.4 us -> none  [the longest x2 15.2 us: gram_sum(): jnp.einsum('mrk,mrl->mkl', block, block, precision=HIGHEST).astype(BF16)]
    all_gather x1 -> x0, waiting for transfers between devices: 36.1 us -> none  [body(): full_m = lax.all_gather(matrices.astype(BF16), 'row', axis=1, tiled=True)]
    unnamed x56, local copies, waits for them, and re-layouts: 4 us -> 16.8 us
  transfers between devices with their start and end apart: 13 -> 4, of which waited for: 8 -> 1; matrix products, arithmetic and copies ran while one was open for 4% -> 2% of each run, Pallas kernels for 1% -> 0%
where the time goes in v2:
time: 327 us; the launch traced here: 326 us
  Pallas kernels  270 us (83%)
  local copies, waits for them, and re-layouts  30.3 us (9%)
  other arithmetic  13.7 us (4%)
  starting transfers between devices  5.39 us (2%)
  waiting for transfers between devices  3.9 us (1%)
    pallas_call x1, Pallas kernels, body(): call(main_kernel, members, [scalars, node_block, node_block, per_member((...  130 us
    pallas_call x1, Pallas kernels, reduce_gradients(): pl.pallas_call(partial(reduce_kernel, depth), in_specs=[hbm, vmem, vmem],...  80.3 us
    pallas_call x1, Pallas kernels, gather_weights(): pl.pallas_call(partial(gather_kernel, depth), in_specs=[vmem, vmem], out_...  32.7 us
    unnamed x56, local copies, waits for them, and re-layouts  16.8 us
    pallas_call x1, Pallas kernels, body(): call(encode_kernel, members, [scalars, per_member((variables, points)), w...  15 us
    pallas_call x1, Pallas kernels, body(): call(encode_back_kernel, members, [scalars, hbm, node_block, per_member((...  12.4 us
  transfers between devices with their start and end apart: 4, of which 1 were waited for; matrix products, arithmetic and copies ran while one was open for 2% of the time, Pallas kernels for 0%

profile of v2, /device:TPU:0, one launch (start us, length us, event | category | flops | bytes accessed | tf_op | source)
XLA Modules:
  0.0 325.9 jit_solution(17124233496081710805)
XLA Ops:
  0.7 1.7 convert.27
  3.0 0.7 reduce_sum.9
  4.3 0.2 concatenate.11
  4.5 1.1 pad_maximum_fusion.block_ref
  5.6 0.6 broadcast_in_dim.19.count_ref
  6.2 32.7 %shard_map.342 = (bf16[8,4,128,512]{3,2,1,0:T(8,128)(2,1)}, f32[8,128]{1,0:T(8,128)}) custom-call(bf16[8,128,512]{2,1,0:T(8,128)(2,1)} %pad_maximum_fusion.block_ref, f32[8,128]{1,0:T(8,128)} %broadcast_in_dim.19.count_ref), custom_call_target="tpu_custom_call" | custom-call | tf_op jit(solution)/shard_map/pallas_call | solution.py:451
  38.9 1.1 slice.43
  40.0 1.0 copy.139
  41.0 15.0 %shard_map.343 = (bf16[3,512,227]{2,1,0:T(8,128)(2,1)}, bf16[3,512,512]{2,1,0:T(8,128)(2,1)}, bf16[3,512,512]{2,1,0:T(8,128)(2,1)}, f32[3,512,512]{2,1,0:T(8,128...) custom-call(s32[3]{0:T(128)} %day_ref.5, ...), custom_call_target="tpu_custom_call" | custom-call | flops 6000000000 | bytes 33554432 | tf_op jit(solution)/shard_map/pallas_call | solution.py:781
  56.1 1.2 fusion.9
  57.3 0.4 collective-permute-start
  57.7 2.3 collective-permute-start.1
  60.2 0.7 copy.126
  60.9 0.7 copy.122
  61.6 0.8 copy.112.varw_ref
  62.4 1.2 slice.50
  64.1 0.7 copy.124
  64.8 0.7 copy.125
  65.5 0.8 copy.120
  66.3 0.7 copy-done.16
  67.1 129.9 %shard_map.344 = (f32[8,512,512]{2,1,0:T(8,128)}, f32[227,512]{1,0:T(8,128)}, f32[227,227]{1,0:T(8,128)}, f32[3,227,1]{2,1,0:T(8,128)}, f32[2,512]{1,0:T(2,128)}...) custom-call(s32[3]{0:T(128)} %day_ref.5, f32[3,512,512]{2,1,0:T(8,128)} %get-tuple-element.38.mesh_ref, ...), custom_call_target="tpu_custom_call" | custom-call | flops 60000002048 | bytes 33554432 | tf_op jit(solution)/shard_map/pallas_call | solution.py:823
  197.0 1.1 fusion.8
  198.1 2.6 collective-permute-start.3
  200.8 0.7 copy.121
  202.2 3.9 %collective-permute-done.2 = bf16[3,64,512]{2,1,0:T(8,128)(2,1)S(1)} collective-permute-done((bf16[3,64,512]{2,1,0:T(8,128)(2,1)S(1)}, bf16[3,64,512]{2,1,0:T(8,128)(2,1)S(1)}, u32[]{:S(2)}, u32[]{:S(2)}) %collective-permute-start.2) | collective-permute-done | bytes 196640 | tf_op jit(solution)/shard_map/ppermute | solution.py:695
  206.1 0.8 pad_maximum_fusion.1.ret_ref
  206.9 12.4 %shard_map.345.slots_ref = f32[8,512,512]{2,1,0:T(8,128)} custom-call(s32[3]{0:T(128)} %day_ref.5, f32[8,512,512]{2,1,0:T(8,128)} %get-tuple-element.41.slots_in_ref, f32[3,512,512]{2,1,0:T(8,128)} %get-tuple-element.42.dmesh_ref, bf16[3,128,512]{2,1,0:T(8,128)(2,1)} %pad_maximum_fusion.1.ret_ref, ...), custom_call_target="tpu_custom_call", output_to_operand_aliasing={{}: (1, {})} | custom-call | flops 4000000000 | bytes 33554432 | tf_op jit(solution)/shard_map/pallas_call | solution.py:902
  219.3 80.3 %shard_map.346 = (f32[8,128,512]{2,1,0:T(8,128)}, bf16[8,128,512]{2,1,0:T(8,128)(2,1)}) custom-call(f32[8,512,512]{2,1,0:T(8,128)} %shard_map.345.slots_ref, f32[7,128,512]{2,1,0:T(8,128)} %momentum_ref.1, f32[8,128]{1,0:T(8,128)} %get-tuple-element.55.count_ref), custom_call_target="tpu_custom_call" | custom-call | tf_op jit(solution)/shard_map/pallas_call | solution.py:647
  299.6 1.7 slice_bitcast_fusion
  301.3 1.0 broadcast_multiply_fusion
  302.2 0.9 divide_subtract_fusion
  303.1 1.8 copy.130
  304.9 1.6 copy.131
  306.6 1.6 copy.132
  308.2 0.8 divide_subtract_fusion.1
  309.0 1.6 copy.127
  310.7 1.6 copy.128
  312.3 1.6 copy.129
  314.0 1.0 divide_subtract_fusion.2
  315.0 0.7 copy.136
  315.7 0.7 copy.137
  316.3 0.7 copy.138
  317.0 1.0 divide_subtract_fusion.3
  318.0 0.7 copy.133
  318.7 0.7 copy.134
  319.3 0.7 copy.135
  320.0 4.6 %multiply_add_fusion = (f32[7,128,512]{2,1,0:T(8,128)}, f32[7,128,512]{2,1,0:T(8,128)}) fusion(f32[8,128,512]{2,1,0:T(8,128)} %get-tuple-element.57, f32[7,128,512]{2,1,0:T(8,128)S(1)} %copy-done, f32[]{:T(128)S(6)} %div.48, bf16[8,128,512]{2,1,0:T(8,128)(2,1)S(1)} %copy-done.1, f32[7,128,512]{2,1,0:T(8,128)} %param.32), kind=kLoop, calls=%fused_computation | loop fusion | flops 3211264 | bytes 10092548 | tf_op jit(solution)/shard_map/add | solution.py:952
  324.6 1.3 slice.61
  (59 shorter events, 1.3 us)
Async XLA Ops:
  0.6 1.8 copy-start.2
  0.7 1.9 copy-start.3
  0.7 2.0 copy-start.9
  0.7 2.2 copy-start.10
  0.7 2.3 copy-start.8
  41.0 20.7 %copy-start.15 = (f32[227]{0:T(256)S(1)}, f32[227]{0:T(256)}, u32[]{:S(2)}) copy-start(f32[227]{0:T(256)} %param.26) | copy-start | bytes 2728
  41.0 22.6 %copy-start.4 = (f32[128,227]{0,1:T(8,128)S(1)}, f32[128,227]{0,1:T(8,128)}, u32[]{:S(2)}) copy-start(f32[128,227]{0,1:T(8,128)} %param.38) | copy-start | bytes 348676
  56.0 7.7 %copy-start.5 = (f32[128,227]{0,1:T(8,128)S(1)}, f32[128,227]{0,1:T(8,128)}, u32[]{:S(2)}) copy-start(f32[128,227]{0,1:T(8,128)} %param.39) | copy-start | bytes 348676
  56.0 7.8 %copy-start.6 = (f32[227,128]{1,0:T(8,128)S(1)}, f32[227,128]{1,0:T(8,128)}, u32[]{:S(2)}) copy-start(f32[227,128]{1,0:T(8,128)} %param.35) | copy-start | bytes 348676
  56.0 7.9 %copy-start.7 = (f32[227,128]{1,0:T(8,128)S(1)}, f32[227,128]{1,0:T(8,128)}, u32[]{:S(2)}) copy-start(f32[227,128]{1,0:T(8,128)} %param.36) | copy-start | bytes 348676
  56.1 8.0 %copy-start.11 = (f32[8,128]{1,0:T(8,128)S(1)}, f32[8,128]{1,0:T(8,128)}, u32[]{:S(2)}) copy-start(f32[8,128]{1,0:T(8,128)} %param.44) | copy-start | bytes 12292
  56.1 8.7 %copy-start.12 = (f32[8,128]{1,0:T(8,128)S(1)}, f32[8,128]{1,0:T(8,128)}, u32[]{:S(2)}) copy-start(f32[8,128]{1,0:T(8,128)} %param.45) | copy-start | bytes 12292
  56.1 9.5 %copy-start.13 = (f32[3,128]{1,0:T(4,128)S(1)}, f32[3,128]{1,0:T(4,128)}, u32[]{:S(2)}) copy-start(f32[3,128]{1,0:T(4,128)} %param.41) | copy-start | bytes 4612
  57.3 9.0 %collective-permute-start = (bf16[3,64,512]{2,1,0:T(8,128)(2,1)S(1)}, bf16[3,64,512]{2,1,0:T(8,128)(2,1)S(1)}, u32[]{:S(2)}, u32[]{:S(2)}) collective-permute-start(bf16[3,64,512]{2,1,0:T(8,128)(2,1)S(1)} %get-tuple-element.121), channel_id=1, source_target_pairs={{0,4},{4,8},{8,12},{12,16},{16,20},{20,24},{24,28},{28,0},{1,5},{5... | collective-permute-start | bytes 589832 | tf_op jit(solution)/shard_map/ppermute | solution.py:695
  57.7 8.6 %collective-permute-start.1 = (bf16[3,64,512]{2,1,0:T(8,128)(2,1)S(1)}, bf16[3,64,512]{2,1,0:T(8,128)(2,1)S(1)}, u32[]{:S(2)}, u32[]{:S(2)}) collective-permute-start(bf16[3,64,512]{2,1,0:T(8,128)(2,1)S(1)} %get-tuple-element.120), channel_id=1, source_target_pairs={{4,0},{8,4},{12,8},{16,12},{20,16},{24,20},{28,24},{0,28},{5,1},{9... | collective-permute-start | bytes 589832 | tf_op jit(solution)/shard_map/ppermute | solution.py:696
  66.3 0.7 copy-start.16
  66.3 0.7 copy-start.17
  67.1 133.7 %copy-start.14 = (f32[3,128]{1,0:T(4,128)S(1)}, f32[3,128]{1,0:T(4,128)}, u32[]{:S(2)}) copy-start(f32[3,128]{1,0:T(4,128)} %param.42) | copy-start | bytes 4612
  198.1 8.0 %collective-permute-start.2 = (bf16[3,64,512]{2,1,0:T(8,128)(2,1)S(1)}, bf16[3,64,512]{2,1,0:T(8,128)(2,1)S(1)}, u32[]{:S(2)}, u32[]{:S(2)}) collective-permute-start(bf16[3,64,512]{2,1,0:T(8,128)(2,1)S(1)} %get-tuple-element.118), channel_id=1, source_target_pairs={{0,4},{4,8},{8,12},{12,16},{16,20},{20,24},{24,28},{28,0},{1,5},{5... | collective-permute-start | bytes 589832 | tf_op jit(solution)/shard_map/ppermute | solution.py:695
  198.1 8.0 %collective-permute-start.3 = (bf16[3,64,512]{2,1,0:T(8,128)(2,1)S(1)}, bf16[3,64,512]{2,1,0:T(8,128)(2,1)S(1)}, u32[]{:S(2)}, u32[]{:S(2)}) collective-permute-start(bf16[3,64,512]{2,1,0:T(8,128)(2,1)S(1)} %get-tuple-element.119), channel_id=1, source_target_pairs={{4,0},{8,4},{12,8},{16,12},{20,16},{24,20},{28,24},{0,28},{5,1},{9... | collective-permute-start | bytes 589832 | tf_op jit(solution)/shard_map/ppermute | solution.py:696
  303.1 16.8 %copy-start = (f32[7,128,512]{2,1,0:T(8,128)S(1)}, f32[7,128,512]{2,1,0:T(8,128)}, u32[]{:S(2)}) copy-start(f32[7,128,512]{2,1,0:T(8,128)} %momentum_ref.1) | copy-start | bytes 5505028
  303.1 16.8 %copy-start.1 = (bf16[8,128,512]{2,1,0:T(8,128)(2,1)S(1)}, bf16[8,128,512]{2,1,0:T(8,128)(2,1)}, u32[]{:S(2)}) copy-start(bf16[8,128,512]{2,1,0:T(8,128)(2,1)} %get-tuple-element.56) | copy-start | bytes 3145732
